TPU v7x, 128 devices: a whole 4x4x4 slice. The times are simulated.
128 devices in a mesh: lat: 8 (over y_hi, z), lon: 16 (over x, y_lo, core).
Axes of the slice: x: 4, y: 4 (y_hi: 2, y_lo: 2; y = y_hi * 2 + y_lo), z: 4, core: 2. Of those that a mesh axis runs over, the one named last changes fastest.
Arguments:
- tokens: bfloat16 [128, 256, 3, 512], P('lat', 'lon'), may hold values from -8 to 8
- w_query: bfloat16 [512, 512], replicated, may hold values from -0.25 to 0.25
- w_key: bfloat16 [512, 512], replicated, may hold values from -0.25 to 0.25
- w_value: bfloat16 [512, 512], replicated, may hold values from -0.25 to 0.25
- w_out: bfloat16 [512, 512], replicated, may hold values from -0.25 to 0.25
- grad_out: bfloat16 [128, 256, 3, 512], P('lat', 'lon'), may hold values from -6 to 6
Outputs:
- grad_tokens: bfloat16 [128, 256, 3, 512], P('lat', 'lon')
- grad_w_query: float32 [512, 512], replicated
- grad_w_key: float32 [512, 512], replicated
- grad_w_value: float32 [512, 512], replicated
- grad_w_out: float32 [512, 512], replicated
All inputs are finite; a program needn't handle non-finite values.
Results may differ from a plain program's by a relative error of at most 0.023.
The roundings to bfloat16 on the way count: a program that leaves them out, or rounds other values in their place, can miss the bound.
Values may be sent and summed in bfloat16 or wider, within the bound.
A program may use at most 128 MiB of HBM per device.

v0:
```python
import jax
import jax.numpy as jnp
from jax import lax
from jax.sharding import PartitionSpec as P

HEADS = 8


rim_width = 6
win_span = 13
tile_edge = 8


def padded(cells, sides, width, closed):
    for axis, dim in sides:
        count = lax.axis_size(axis)
        ends = count if closed else count - 1
        head = lax.slice_in_dim(cells, 0, width, axis=dim)
        tail = lax.slice_in_dim(cells, cells.shape[dim] - width, cells.shape[dim], axis=dim)
        cells = jnp.concatenate(
            [
                lax.ppermute(tail, axis, [(i, (i + 1) % count) for i in range(ends)]),
                cells,
                lax.ppermute(head, axis, [((i + 1) % count, i) for i in range(ends)]),
            ],
            axis=dim,
        )
    return cells


def tile_mask(row_start, lat_total, levels):
    fill_query = jnp.zeros((tile_edge, tile_edge, levels), jnp.int32)
    query_row = (jnp.arange(tile_edge, dtype=jnp.int32)[:, None, None] + fill_query).reshape(-1)
    query_col = (jnp.arange(tile_edge, dtype=jnp.int32)[None, :, None] + fill_query).reshape(-1)
    tile_span = tile_edge + 2 * rim_width
    fill_key = jnp.zeros((tile_span, tile_span, levels), jnp.int32)
    key_row = (jnp.arange(tile_span, dtype=jnp.int32)[:, None, None] + fill_key).reshape(-1)
    key_col = (jnp.arange(tile_span, dtype=jnp.int32)[None, :, None] + fill_key).reshape(-1)
    query_lat = row_start + query_row
    window_start = jnp.clip(query_lat - rim_width, 0, lat_total - win_span)
    key_lat = row_start - rim_width + key_row
    lat_inside = (key_lat[None, :] >= window_start[:, None]) & (
        key_lat[None, :] < window_start[:, None] + win_span
    )
    offset = key_col[None, :] - rim_width - query_col[:, None]
    lon_inside = jnp.abs(offset) <= rim_width
    return lat_inside & lon_inside


def tile_grad(queries, keyvals, upstream, allowed, head_count):
    model_width = queries.shape[1]
    head_dim = model_width // head_count
    score_scale = head_dim ** (-0.5)
    query_count = queries.shape[0]
    q_heads = queries.reshape(query_count, head_count, head_dim)
    k_heads = keyvals[:, :model_width].reshape(-1, head_count, head_dim)
    v_heads = keyvals[:, model_width:].reshape(-1, head_count, head_dim)
    g_heads = upstream.reshape(query_count, head_count, head_dim)
    scores = (
        jnp.einsum("qhd,khd->hqk", q_heads, k_heads, preferred_element_type=jnp.float32)
        * score_scale
    )
    scores = jnp.where(allowed[None], scores, -jnp.inf)
    row_max = jnp.max(scores, axis=-1, keepdims=True)
    shifted = jnp.exp(scores - row_max)
    totals = jnp.sum(shifted, axis=-1, keepdims=True)
    attn_prob = shifted / totals
    log_norm = (row_max + jnp.log(totals))[:, :, 0].T
    prob_low = attn_prob.astype(jnp.bfloat16)
    attended = jnp.einsum(
        "hqk,khd->qhd", prob_low, v_heads, preferred_element_type=jnp.float32
    ).astype(jnp.bfloat16)
    row_dot = jnp.sum(g_heads.astype(jnp.float32) * attended.astype(jnp.float32), axis=-1)
    grad_prob = jnp.einsum("qhd,khd->hqk", g_heads, v_heads, preferred_element_type=jnp.float32)
    grad_score = (attn_prob * (grad_prob - row_dot.T[:, :, None])).astype(jnp.bfloat16)
    grad_query = (
        jnp.einsum("hqk,khd->qhd", grad_score, k_heads, preferred_element_type=jnp.float32)
        * score_scale
    )
    grad_key = (
        jnp.einsum("hqk,qhd->khd", grad_score, q_heads, preferred_element_type=jnp.float32)
        * score_scale
    )
    grad_value = jnp.einsum("hqk,qhd->khd", prob_low, g_heads, preferred_element_type=jnp.float32)
    key_count = keyvals.shape[0]
    grad_kv = jnp.concatenate(
        [grad_key.reshape(key_count, model_width), grad_value.reshape(key_count, model_width)],
        axis=1,
    )
    row_stats = jnp.concatenate([log_norm, row_dot], axis=1)
    return (
        attended.reshape(query_count, model_width),
        grad_query.reshape(query_count, model_width),
        grad_kv,
        row_stats,
    )


def project(flat_rows, weight):
    return jnp.dot(flat_rows, weight, preferred_element_type=jnp.float32).astype(jnp.bfloat16)


def on_device(tokens, w_query, w_key, w_value, w_out, grad_out):
    lat_dev, lon_dev, levels, model_width = tokens.shape
    block_shape = tokens.shape
    flat_tokens = tokens.reshape(-1, model_width)
    flat_grad = grad_out.reshape(-1, model_width)
    query = project(flat_tokens, w_query).reshape(block_shape)
    upstream = (
        jnp.einsum("te,de->td", flat_grad, w_out, preferred_element_type=jnp.float32)
        .astype(jnp.bfloat16)
        .reshape(block_shape)
    )
    wide_shape = (lat_dev + 2 * rim_width, lon_dev + 2 * rim_width, levels, 2 * model_width)
    local_kv = jnp.concatenate([project(flat_tokens, w_key), project(flat_tokens, w_value)], axis=1)
    local_kv = local_kv.reshape(lat_dev, lon_dev, levels, 2 * model_width)
    wide_kv = padded(local_kv, (("lon", 1),), rim_width, True)
    keyvals = padded(wide_kv, (("lat", 0),), rim_width, False)
    lat_total = lat_dev * lax.axis_size("lat")
    lat_offset = lax.axis_index("lat") * lat_dev
    tiles_lon = lon_dev // tile_edge
    tile_count = lat_dev // tile_edge * tiles_lon
    tile_span = tile_edge + 2 * rim_width
    zero_index = jnp.zeros((), jnp.int32)

    def one_tile(index, carry):
        attended_all, grad_query_all, extra_all = carry
        index = jnp.asarray(index).astype(jnp.int32)
        row_first = index // tiles_lon * tile_edge
        col_first = index % tiles_lon * tile_edge
        starts = (row_first, col_first, zero_index, zero_index)
        query_tile = lax.dynamic_slice(
            query, starts, (tile_edge, tile_edge, levels, model_width)
        ).reshape(-1, model_width)
        upstream_tile = lax.dynamic_slice(
            upstream, starts, (tile_edge, tile_edge, levels, model_width)
        ).reshape(-1, model_width)
        kv_tile = lax.dynamic_slice(
            keyvals, starts, (tile_span, tile_span, levels, 2 * model_width)
        ).reshape(-1, 2 * model_width)
        allowed = tile_mask(lat_offset + row_first, lat_total, levels)
        attended, grad_query, grad_kv, row_stats = tile_grad(
            query_tile, kv_tile, upstream_tile, allowed, HEADS
        )
        attended_all = lax.dynamic_update_slice(
            attended_all, attended.reshape(tile_edge, tile_edge, levels, model_width), starts
        )
        grad_query_all = lax.dynamic_update_slice(
            grad_query_all, grad_query.reshape(tile_edge, tile_edge, levels, model_width), starts
        )
        previous = lax.dynamic_slice(
            extra_all, starts, (tile_span, tile_span, levels, 2 * model_width)
        )
        extra_all = lax.dynamic_update_slice(
            extra_all,
            previous + grad_kv.reshape(tile_span, tile_span, levels, 2 * model_width),
            starts,
        )
        return (attended_all, grad_query_all, extra_all)

    extra_init = jnp.zeros(wide_shape, jnp.float32)
    initial = (
        jnp.zeros(block_shape, jnp.bfloat16),
        jnp.zeros(block_shape, jnp.float32),
        extra_init,
    )
    attended_all, grad_query_all, extra_all = lax.fori_loop(0, tile_count, one_tile, initial)
    part_out = jnp.einsum(
        "td,te->de",
        attended_all.reshape(-1, model_width),
        flat_grad,
        preferred_element_type=jnp.float32,
    )
    returned = padded(extra_all, (("lat", 0),), rim_width, False)
    core = returned[2 * rim_width : 2 * rim_width + lat_dev]
    core = core.at[:rim_width].add(returned[:rim_width])
    core = core.at[lat_dev - rim_width :].add(returned[lat_dev + 3 * rim_width :])
    returned = padded(core, (("lon", 1),), rim_width, True)
    owned = returned[:, 2 * rim_width : 2 * rim_width + lon_dev]
    owned = owned.at[:, :rim_width].add(returned[:, :rim_width])
    owned = owned.at[:, lon_dev - rim_width :].add(returned[:, lon_dev + 3 * rim_width :])
    grad_query_low = grad_query_all.astype(jnp.bfloat16).reshape(-1, model_width)
    grad_key_low = owned[..., :model_width].astype(jnp.bfloat16).reshape(-1, model_width)
    grad_value_low = owned[..., model_width:].astype(jnp.bfloat16).reshape(-1, model_width)
    grad_tokens = jnp.einsum(
        "te,de->td", grad_query_low, w_query, preferred_element_type=jnp.float32
    )
    grad_tokens = grad_tokens + jnp.einsum(
        "te,de->td", grad_key_low, w_key, preferred_element_type=jnp.float32
    )
    grad_tokens = grad_tokens + jnp.einsum(
        "te,de->td", grad_value_low, w_value, preferred_element_type=jnp.float32
    )
    grad_tokens = grad_tokens.astype(jnp.bfloat16).reshape(block_shape)
    part_query = jnp.einsum(
        "td,te->de", flat_tokens, grad_query_low, preferred_element_type=jnp.float32
    )
    part_key = jnp.einsum(
        "td,te->de", flat_tokens, grad_key_low, preferred_element_type=jnp.float32
    )
    part_value = jnp.einsum(
        "td,te->de", flat_tokens, grad_value_low, preferred_element_type=jnp.float32
    )
    total_query, total_key, total_value, total_out = lax.psum(
        (part_query, part_key, part_value, part_out), ("lat", "lon")
    )
    return (grad_tokens, total_query, total_key, total_value, total_out)


def solution(mesh):
    placed = (P("lat", "lon", None, None), P(), P(), P(), P(), P("lat", "lon", None, None))
    return jax.shard_map(
        on_device,
        mesh=mesh,
        in_specs=placed,
        out_specs=(P("lat", "lon", None, None), P(), P(), P(), P()),
        check_vma=False,
    )
```

profile of v0, /device:TPU:1, one launch (start us, length us, event | category | flops | bytes accessed | tf_op | source)
XLA Modules:
  0.0 865.4 jit_solution(7626926816751982139)
XLA Ops:
  21.3 12.6 %collective-permute-done = bf16[16,6,3,1024]{3,0,2,1:T(8,128)(2,1)S(1)} collective-permute-done((bf16[16,6,3,1024]{3,0,2,1:T(8,128)(2,1)S(1)}, bf16[16,6,3,1024]{3,0,2,1:T(8,128)(2,1)S(1)}, u32[]{:S(2)}, u32[]{:S(2)}) %collective-permute-start) | collective-permute-done | bytes 589856 | tf_op jit(solution)/shard_map/ppermute | solution.py:22
  61.1 5.8 collective-permute-done.3
  85.8 486.3 %while.24 = (s32[]{:T(128)}, bf16[16,16,3,512]{3,1,2,0:T(8,128)(2,1)}, bf16[16,16,3,512]{3,2,1,0:T(4,128)(2,1)}, f32[28,28,3,1024]{3,1,2,0:T(8,128)}, bf16[28,28...) while((s32[]{:T(128)}, ...), condition=%wide.region_4.5_spmd, body=%wide.region_0.4_spmd.sunk | while | flops 1439385344 | bytes 207698448 | solution.py:167
  107.8 6.1 reshape.477
  122.0 7.0 fusion.90
  156.5 6.5 concatenate.38
  169.8 6.4 concatenate.39
  186.3 6.5 copy.125
  192.8 26.2 %dynamic_update_slice.40 = f32[28,28,3,1024]{3,1,2,0:T(8,128)} dynamic-update-slice(f32[28,28,3,1024]{3,1,2,0:T(8,128)} %get-tuple-element.436, f32[20,20,3,1024]{3,1,2,0:T(8,128)} %copy.125, s32[]{:T(128)S(6)} %select_n.117, s32[]{:T(128)S(6)} %select_n.118, s32[]{:T(128)} %constant.283.clone.1..sunk, s32[]{:T(128)} %constant.283.clone.1..sunk) | dynamic-update-slice | bytes 9830404 | tf_op jit(solution)/shard_map/while/body/eval_jaxpr/dynamic_update_slice | solution.py:154
  226.0 6.1 reshape.477
  240.2 7.0 fusion.90
  274.7 6.5 concatenate.38
  288.0 6.4 concatenate.39
  304.0 6.5 copy.125
  310.5 25.7 %dynamic_update_slice.40 = f32[28,28,3,1024]{3,1,2,0:T(8,128)} dynamic-update-slice(f32[28,28,3,1024]{3,1,2,0:T(8,128)} %get-tuple-element.436, f32[20,20,3,1024]{3,1,2,0:T(8,128)} %copy.125, s32[]{:T(128)S(6)} %select_n.117, s32[]{:T(128)S(6)} %select_n.118, s32[]{:T(128)} %constant.283.clone.1..sunk, s32[]{:T(128)} %constant.283.clone.1..sunk) | dynamic-update-slice | bytes 9830404 | tf_op jit(solution)/shard_map/while/body/eval_jaxpr/dynamic_update_slice | solution.py:154
  343.2 6.1 reshape.477
  357.4 7.0 fusion.90
  391.9 6.5 concatenate.38
  405.2 6.4 concatenate.39
  421.8 6.5 copy.125
  428.3 26.2 %dynamic_update_slice.40 = f32[28,28,3,1024]{3,1,2,0:T(8,128)} dynamic-update-slice(f32[28,28,3,1024]{3,1,2,0:T(8,128)} %get-tuple-element.436, f32[20,20,3,1024]{3,1,2,0:T(8,128)} %copy.125, s32[]{:T(128)S(6)} %select_n.117, s32[]{:T(128)S(6)} %select_n.118, s32[]{:T(128)} %constant.283.clone.1..sunk, s32[]{:T(128)} %constant.283.clone.1..sunk) | dynamic-update-slice | bytes 9830404 | tf_op jit(solution)/shard_map/while/body/eval_jaxpr/dynamic_update_slice | solution.py:154
  461.5 6.1 reshape.477
  475.7 7.0 fusion.90
  510.2 6.5 concatenate.38
  523.5 6.4 concatenate.39
  539.5 6.5 copy.125
  546.0 25.7 %dynamic_update_slice.40 = f32[28,28,3,1024]{3,1,2,0:T(8,128)} dynamic-update-slice(f32[28,28,3,1024]{3,1,2,0:T(8,128)} %get-tuple-element.436, f32[20,20,3,1024]{3,1,2,0:T(8,128)} %copy.125, s32[]{:T(128)S(6)} %select_n.117, s32[]{:T(128)S(6)} %select_n.118, s32[]{:T(128)} %constant.283.clone.1..sunk, s32[]{:T(128)} %constant.283.clone.1..sunk) | dynamic-update-slice | bytes 9830404 | tf_op jit(solution)/shard_map/while/body/eval_jaxpr/dynamic_update_slice | solution.py:154
  583.5 43.9 %collective-permute-done.4 = f32[6,28,3,1024]{3,1,2,0:T(8,128)S(1)} collective-permute-done((f32[6,28,3,1024]{3,1,2,0:T(8,128)S(1)}, f32[6,28,3,1024]{3,1,2,0:T(8,128)S(1)}, u32[]{:S(2)}, u32[]{:S(2)}) %collective-permute-start.4) | collective-permute-done | bytes 2064416 | tf_op jit(solution)/shard_map/ppermute | solution.py:22
  641.3 18.2 %collective-permute-done.6 = f32[16,6,3,1024]{3,0,2,1:T(8,128)S(1)} collective-permute-done((f32[16,6,3,1024]{3,0,2,1:T(8,128)S(1)}, f32[16,6,3,1024]{3,0,2,1:T(8,128)S(1)}, u32[]{:S(2)}, u32[]{:S(2)}) %collective-permute-start.6) | collective-permute-done | bytes 1179680 | tf_op jit(solution)/shard_map/ppermute | solution.py:22
  660.5 8.4 scatter-add.16
  671.6 7.6 scatter-add.19
  699.6 151.3 %all-reduce.3.cloned.1.call-done = (f32[512,512]{0,1:T(8,128)}, f32[512,512]{0,1:T(8,128)}, f32[512,512]{0,1:T(8,128)}, f32[512,512]{1,0:T(8,128)}) async-done(((f32[512,512]{0,1:T(8,128)}, f32[512,512]{0,1:T(8,128)}, f32[512,512]{0,1:T(8,128)}, f32[512,512]{1,0:T(8,128)}), (f32[512,512]{0,1:T(8,128)}, f32[512,512]{0,1:T(8,128)}, f32[512,512]{0,1:T(8,128)}, ...) | async-done | bytes 4194320 | tf_op jit(solution)/shard_map/psum | solution.py:204
  (324 shorter events, 352.9 us)
Async XLA Ops:
  7.2 41.6 %copy-start = (bf16[512,512]{1,0:T(8,128)(2,1)S(1)}, bf16[512,512]{1,0:T(8,128)(2,1)}, u32[]{:S(2)}) copy-start(bf16[512,512]{1,0:T(8,128)(2,1)} %param.17) | copy-start | bytes 1572868
  7.2 843.7 %all-reduce.3.cloned.1.call-start = ((), (), s32[]{:S(2)}) async-start(), calls=%async_computation | async-start | bytes 8388608 | tf_op jit(solution)/shard_map/psum | solution.py:204
  18.0 15.9 %collective-permute-start = (bf16[16,6,3,1024]{3,0,2,1:T(8,128)(2,1)S(1)}, bf16[16,6,3,1024]{3,0,2,1:T(8,128)(2,1)S(1)}, u32[]{:S(2)}, u32[]{:S(2)}) collective-permute-start(bf16[16,6,3,1024]{3,0,2,1:T(8,128)(2,1)S(1)} %copy.62), channel_id=1, source_target_pairs={{0,1},{1,2},{2,3},{3,4},{4,5},{5,6},{6,7},{7,8},{8,9},{9,10},{10,1... | collective-permute-start | bytes 1769480 | tf_op jit(solution)/shard_map/ppermute | solution.py:22
  21.2 15.3 %collective-permute-start.1 = (bf16[16,6,3,1024]{3,0,2,1:T(8,128)(2,1)S(1)}, bf16[16,6,3,1024]{3,0,2,1:T(8,128)(2,1)S(1)}, u32[]{:S(2)}, u32[]{:S(2)}) collective-permute-start(bf16[16,6,3,1024]{3,0,2,1:T(8,128)(2,1)S(1)} %copy.63), channel_id=1, source_target_pairs={{1,0},{2,1},{3,2},{4,3},{5,4},{6,5},{7,6},{8,7},{9,8},{10,9},{11,1... | collective-permute-start | bytes 1769480 | tf_op jit(solution)/shard_map/ppermute | solution.py:24
  40.3 26.5 %collective-permute-start.3 = (bf16[6,28,3,1024]{3,1,2,0:T(8,128)(2,1)}, bf16[6,28,3,1024]{3,1,2,0:T(8,128)(2,1)}, u32[]{:S(2)}, u32[]{:S(2)}) collective-permute-start(bf16[6,28,3,1024]{3,1,2,0:T(8,128)(2,1)} %copy.67), channel_id=1, source_target_pairs={{16,0},{32,16},{48,32},{64,48},{80,64},{96,80},{112,96},{17,1},{33... | collective-permute-start | bytes 3096584 | tf_op jit(solution)/shard_map/ppermute | solution.py:24
  43.0 27.0 %collective-permute-start.2 = (bf16[6,28,3,1024]{3,1,2,0:T(8,128)(2,1)}, bf16[6,28,3,1024]{3,1,2,0:T(8,128)(2,1)}, u32[]{:S(2)}, u32[]{:S(2)}) collective-permute-start(bf16[6,28,3,1024]{3,1,2,0:T(8,128)(2,1)} %copy.66), channel_id=1, source_target_pairs={{0,16},{16,32},{32,48},{48,64},{64,80},{80,96},{96,112},{1,17},{17... | collective-permute-start | bytes 3096584 | tf_op jit(solution)/shard_map/ppermute | solution.py:22
  50.2 5.8 copy-start.25
  61.1 11.1 %copy-start.8 = (bf16[16,28,3,1024]{3,2,1,0:T(4,128)(2,1)S(1)}, bf16[16,28,3,1024]{3,2,1,0:T(4,128)(2,1)}, u32[]{:S(2)}) copy-start(bf16[16,28,3,1024]{3,2,1,0:T(4,128)(2,1)} %copy-done.7) | copy-start | bytes 8257540
  156.5 6.5 copy-start.6
  176.1 4.4 copy-start.3
  176.1 5.2 copy-start.4
  192.8 26.2 %copy-start.11 = (bf16[16,16,3,512]{3,2,1,0:T(4,128)(2,1)S(1)}, bf16[16,16,3,512]{3,2,1,0:T(4,128)(2,1)}, u32[]{:S(2)}) copy-start(bf16[16,16,3,512]{3,2,1,0:T(4,128)(2,1)} %copy-done.10) | copy-start | bytes 2359300 | tf_op jit(solution)/shard_map/while
  192.8 26.2 %copy-start.13 = (bf16[16,16,3,512]{3,2,1,0:T(4,128)(2,1)S(1)}, bf16[16,16,3,512]{3,2,1,0:T(4,128)(2,1)}, u32[]{:S(2)}) copy-start(bf16[16,16,3,512]{3,2,1,0:T(4,128)(2,1)} %copy-done.12) | copy-start | bytes 2359300 | tf_op jit(solution)/shard_map/while
  274.7 6.5 copy-start.6
  294.4 4.6 copy-start.4
  310.5 25.7 %copy-start.11 = (bf16[16,16,3,512]{3,2,1,0:T(4,128)(2,1)S(1)}, bf16[16,16,3,512]{3,2,1,0:T(4,128)(2,1)}, u32[]{:S(2)}) copy-start(bf16[16,16,3,512]{3,2,1,0:T(4,128)(2,1)} %copy-done.10) | copy-start | bytes 2359300 | tf_op jit(solution)/shard_map/while
  310.5 25.7 %copy-start.13 = (bf16[16,16,3,512]{3,2,1,0:T(4,128)(2,1)S(1)}, bf16[16,16,3,512]{3,2,1,0:T(4,128)(2,1)}, u32[]{:S(2)}) copy-start(bf16[16,16,3,512]{3,2,1,0:T(4,128)(2,1)} %copy-done.12) | copy-start | bytes 2359300 | tf_op jit(solution)/shard_map/while
  391.9 6.5 copy-start.6
  411.6 4.4 copy-start.3
  411.6 5.2 copy-start.4
  428.3 26.2 %copy-start.11 = (bf16[16,16,3,512]{3,2,1,0:T(4,128)(2,1)S(1)}, bf16[16,16,3,512]{3,2,1,0:T(4,128)(2,1)}, u32[]{:S(2)}) copy-start(bf16[16,16,3,512]{3,2,1,0:T(4,128)(2,1)} %copy-done.10) | copy-start | bytes 2359300 | tf_op jit(solution)/shard_map/while
  428.3 26.2 %copy-start.13 = (bf16[16,16,3,512]{3,2,1,0:T(4,128)(2,1)S(1)}, bf16[16,16,3,512]{3,2,1,0:T(4,128)(2,1)}, u32[]{:S(2)}) copy-start(bf16[16,16,3,512]{3,2,1,0:T(4,128)(2,1)} %copy-done.12) | copy-start | bytes 2359300 | tf_op jit(solution)/shard_map/while
  510.2 6.5 copy-start.6
  529.8 4.6 copy-start.4
  546.0 25.7 %copy-start.11 = (bf16[16,16,3,512]{3,2,1,0:T(4,128)(2,1)S(1)}, bf16[16,16,3,512]{3,2,1,0:T(4,128)(2,1)}, u32[]{:S(2)}) copy-start(bf16[16,16,3,512]{3,2,1,0:T(4,128)(2,1)} %copy-done.10) | copy-start | bytes 2359300 | tf_op jit(solution)/shard_map/while
  546.0 25.7 %copy-start.13 = (bf16[16,16,3,512]{3,2,1,0:T(4,128)(2,1)S(1)}, bf16[16,16,3,512]{3,2,1,0:T(4,128)(2,1)}, u32[]{:S(2)}) copy-start(bf16[16,16,3,512]{3,2,1,0:T(4,128)(2,1)} %copy-done.12) | copy-start | bytes 2359300 | tf_op jit(solution)/shard_map/while
  574.8 52.6 %collective-permute-start.4 = (f32[6,28,3,1024]{3,1,2,0:T(8,128)S(1)}, f32[6,28,3,1024]{3,1,2,0:T(8,128)S(1)}, u32[]{:S(2)}, u32[]{:S(2)}) collective-permute-start(f32[6,28,3,1024]{3,1,2,0:T(8,128)S(1)} %get-tuple-element.343), channel_id=1, source_target_pairs={{0,16},{16,32},{32,48},{48,64},{64,80},{80,96},{96,112},{1,17},{17... | collective-permute-start | bytes 6193160 | tf_op jit(solution)/shard_map/ppermute | solution.py:22
  578.8 52.9 %collective-permute-start.5 = (f32[6,28,3,1024]{3,1,2,0:T(8,128)S(1)}, f32[6,28,3,1024]{3,1,2,0:T(8,128)S(1)}, u32[]{:S(2)}, u32[]{:S(2)}) collective-permute-start(f32[6,28,3,1024]{3,1,2,0:T(8,128)S(1)} %get-tuple-element.342), channel_id=1, source_target_pairs={{16,0},{32,16},{48,32},{64,48},{80,64},{96,80},{112,96},{17,1},{33... | collective-permute-start | bytes 6193160 | tf_op jit(solution)/shard_map/ppermute | solution.py:24
  633.7 25.9 %collective-permute-start.6 = (f32[16,6,3,1024]{3,0,2,1:T(8,128)S(1)}, f32[16,6,3,1024]{3,0,2,1:T(8,128)S(1)}, u32[]{:S(2)}, u32[]{:S(2)}) collective-permute-start(f32[16,6,3,1024]{3,0,2,1:T(8,128)S(1)} %copy.75), channel_id=1, source_target_pairs={{0,1},{1,2},{2,3},{3,4},{4,5},{5,6},{6,7},{7,8},{8,9},{9,10},{10,1... | collective-permute-start | bytes 3538952 | tf_op jit(solution)/shard_map/ppermute | solution.py:22
  635.5 33.5 %collective-permute-start.7 = (f32[16,6,3,1024]{3,0,2,1:T(8,128)}, f32[16,6,3,1024]{3,0,2,1:T(8,128)}, u32[]{:S(2)}, u32[]{:S(2)}) collective-permute-start(f32[16,6,3,1024]{3,0,2,1:T(8,128)} %copy.77), channel_id=1, source_target_pairs={{1,0},{2,1},{3,2},{4,3},{5,4},{6,5},{7,6},{8,7},{9,8},{10,9},{11,1... | collective-permute-start | bytes 3538952 | tf_op jit(solution)/shard_map/ppermute | solution.py:24
  850.9 5.2 copy-start.17
  853.5 3.9 copy-start.16
  (33 other events, 76.6 us)
Sparse Core Ops, SparseCore 0:
  684.7 166.1 all-reduce.2
where the time goes:
time: 879 us; the launch traced here: 865 us
  local copies, waits for them, and re-layouts  428 us (49%)
  waiting for transfers between devices  236 us (27%)
  matrix products  99.2 us (11%)
  other arithmetic  55.8 us (6%)
  loops' own time  16.5 us (2%)
  starting transfers between devices  15.7 us (2%)
  between operations  14.6 us (2%)
    psum x1, waiting for transfers between devices, on_device(): lax.psum((part_query, part_key, part_value, part_out), ('lat', 'lon'))  151 us
    dynamic_update_slice x8, local copies, waits for them, and re-layouts, one_tile(): lax.dynamic_update_slice(extra_all, previous + grad_kv.reshape(tile_span,...  130 us
    ppermute x4, waiting for transfers between devices, padded(): lax.ppermute(tail, axis, [(i, (i + 1) % count) for i in range(ends)])  75.8 us
    concatenate x8, local copies, waits for them, and re-layouts, tile_grad(): jnp.concatenate([grad_key.reshape(key_count, model_width), grad_value.res...  51.3 us
    sub x4, matrix products, tile_grad(): shifted = jnp.exp(scores - row_max)  28.2 us
    reshape x4, local copies, waits for them, and re-layouts, one_tile(): kv_tile = lax.dynamic_slice(keyvals, starts, (tile_span, tile_span, level...  24.4 us
    dynamic_slice x4, local copies, waits for them, and re-layouts, one_tile(): lax.dynamic_slice(keyvals, starts, (tile_span, tile_span, levels, 2 * mod...  21.1 us
    add x4, other arithmetic, one_tile(): previous + grad_kv.reshape(tile_span, tile_span, levels, 2 * model_width)  20 us
  transfers between devices with their start and end apart: 9, of which 8 were waited for; matrix products, arithmetic and copies ran while one was open for 6% of the time, Pallas kernels for 0%

commit v1 on v0

v1 whole, which is shorter than its diff:
```python
import functools

import jax
import jax.numpy as jnp
from jax import lax
from jax.experimental import pallas as pl
from jax.experimental.pallas import tpu as pltpu
from jax.sharding import PartitionSpec as P

HEADS = 8
HEAD = 64
D = 512
RIM = 6
SPAN = 13
OWN = 28 * 48
SIDE = 28 * 24
ALL = OWN + 2 * SIDE
TQ = 96
KEYS = 768 + 384
CHUNK = 384
F32 = jnp.float32
BF16 = jnp.bfloat16


def nn(a, b):
    return jnp.dot(a, b, preferred_element_type=F32)


def nt(a, b):
    return lax.dot_general(a, b, (((1,), (1,)), ((), ())), preferred_element_type=F32)


def tn(a, b):
    return lax.dot_general(a, b, (((0,), (0,)), ((), ())), preferred_element_type=F32)


def attention_kernel(
    lat_total,
    row0_ref,
    tok_ref,
    grad_ref,
    wq_ref,
    wk_ref,
    wv_ref,
    wo_ref,
    gt_own_ref,
    gt_wide_ref,
    gwq_ref,
    gwk_ref,
    gwv_ref,
    gwo_ref,
    k_ref,
    v_ref,
    kt_ref,
    vt_ref,
    q_ref,
    u_ref,
    gk_ref,
    gv_ref,
    gq_ref,
    att_ref,
    qbd_ref,
    ubd_ref,
    ubdt_ref,
    bias_ref,
    s_ref,
    p_ref,
):
    row0 = row0_ref[0]
    own_rows = pl.ds(RIM * 48, 768)

    def project(i, carry):
        rows = pl.ds(pl.multiple_of(i * 192, 192), 192)
        x = tok_ref[rows, :]
        k_ref[rows, :] = nn(x, wk_ref[...]).astype(BF16)
        v_ref[rows, :] = nn(x, wv_ref[...]).astype(BF16)
        gk_ref[rows, :] = jnp.zeros((192, D), F32)
        gv_ref[rows, :] = jnp.zeros((192, D), F32)
        return carry

    lax.fori_loop(0, ALL // 192, project, 0)
    for i in range(4):
        x = tok_ref[pl.ds(RIM * 48 + 192 * i, 192), :]
        q = nn(x, wq_ref[...]).astype(BF16).astype(F32) * 0.125
        q_ref[pl.ds(12 * i, 12)] = q.reshape(12, 16, D)
        g = grad_ref[pl.ds(192 * i, 192), :]
        u = nt(g, wo_ref[...]).astype(BF16).astype(F32)
        u_ref[pl.ds(12 * i, 12)] = u.reshape(12, 16, D)

    head_row = lax.broadcasted_iota(jnp.int32, (256, 256), 0)
    feature = lax.broadcasted_iota(jnp.int32, (256, 256), 1)

    def diagonal(n):
        owner = (head_row + 256 * n) // TQ
        return owner == (feature + 128 * n) // HEAD

    def latitude_band(r, carry):
        lowest = jnp.where(row0 == 0, RIM, 0)
        highest = jnp.where(row0 + 16 == lat_total, RIM, 12)
        base = jnp.clip(4 * r, lowest, highest)
        for i in range(2):
            part = pl.ds(pl.multiple_of(base * 48 + 384 * i, 48), 384)
            kt_ref[:, pl.ds(384 * i, 384)] = k_ref[part, :].T
            vt_ref[:, pl.ds(384 * i, 384)] = v_ref[part, :].T
        for c in range(2):
            part = pl.ds(pl.multiple_of(OWN + SIDE * c + base * 24, 48), 384)
            kt_ref[:, pl.ds(768 + 384 * c, 384)] = k_ref[part, :].T
            vt_ref[:, pl.ds(768 + 384 * c, 384)] = v_ref[part, :].T

        for c in range(2):
            starts = [
                pl.multiple_of(base * 48, 48),
                pl.multiple_of(base * 48 + 384, 48),
                pl.multiple_of(OWN + SIDE * c + base * 24, 48),
            ]
            columns = [0, 384, 768 + 384 * c]

            lane = lax.broadcasted_iota(jnp.int32, (1, 512), 1) % TQ
            q_lat = row0 + 4 * r + lane // 24
            first = jnp.clip(q_lat - RIM, 0, lat_total - SPAN) - (row0 + base - RIM)
            q_col = lane % 8
            key = lax.broadcasted_iota(jnp.int32, (768, 1), 0)
            d_lat = key // 48 - first
            d_col = key % 16 - 8 * c - q_col + RIM
            inside = (d_lat >= 0) & (d_lat < SPAN) & (d_col >= 0) & (d_col < SPAN)
            bias_ref[0:768, :] = jnp.where(inside, 0.0, -jnp.inf)
            key = lax.broadcasted_iota(jnp.int32, (384, 1), 0)
            d_lat = key // 24 - first
            d_col = key % 8 + (16 * c - 8) - q_col + RIM
            inside = (d_lat >= 0) & (d_lat < SPAN) & (d_col >= 0) & (d_col < SPAN)
            bias_ref[768:1152, :] = jnp.where(inside, 0.0, -jnp.inf)

            groups = pl.ds(12 * r, 12)
            q_tile = q_ref[groups, 8 * c : 8 * c + 8, :].reshape(TQ, D).astype(BF16)
            u_tile = u_ref[groups, 8 * c : 8 * c + 8, :].reshape(TQ, D).astype(BF16)
            q_all = jnp.concatenate([q_tile] * HEADS, axis=0)
            u_all = jnp.concatenate([u_tile] * HEADS, axis=0)
            for n in range(3):
                keep = diagonal(n)
                block = q_all[256 * n : 256 * n + 256, 128 * n : 128 * n + 256]
                qbd_ref[n] = jnp.where(keep, block, jnp.zeros_like(block))
                block = u_all[256 * n : 256 * n + 256, 128 * n : 128 * n + 256]
                block = jnp.where(keep, block, jnp.zeros_like(block))
                ubd_ref[n] = block
                ubdt_ref[n] = block.astype(F32).T

            att_parts = [None] * HEADS
            gq_parts = [None] * HEADS

            def fold(parts, n, block):
                block = jnp.where(diagonal(n), block, 0.0)
                row = 256 * n
                while row < 256 * n + 256:
                    h = row // TQ
                    end = min(TQ * (h + 1), 256 * n + 256)
                    piece = block[row - 256 * n : end - 256 * n]
                    parts.append((row - TQ * h, end - TQ * h, n, piece))
                    row = end

            att_parts = []
            gq_parts = []
            for n in range(3):
                feats = pl.ds(128 * n, 256)
                bias_lane = (0, 256, 128)[n]
                high = jnp.full((8, 256), -jnp.inf, F32)
                for j in range(3):
                    rows = pl.ds(starts[j], CHUNK)
                    s = nt(k_ref[rows, feats], qbd_ref[n])
                    s = s + bias_ref[pl.ds(CHUNK * j, CHUNK), pl.ds(bias_lane, 256)]
                    s_ref[pl.ds(CHUNK * j, CHUNK), :] = s
                    high = jnp.maximum(high, jnp.max(s.reshape(CHUNK // 8, 8, 256), axis=0))
                high = jnp.max(high, axis=0, keepdims=True)
                total = jnp.zeros((8, 256), F32)
                for j in range(3):
                    part = pl.ds(CHUNK * j, CHUNK)
                    e = jnp.exp(s_ref[part, :] - high)
                    s_ref[part, :] = e
                    total = total + jnp.sum(e.reshape(CHUNK // 8, 8, 256), axis=0)
                scale = 1.0 / jnp.sum(total, axis=0, keepdims=True)
                out_t = jnp.zeros((256, 256), F32)
                for j in range(3):
                    part = pl.ds(CHUNK * j, CHUNK)
                    p = s_ref[part, :] * scale
                    s_ref[part, :] = p
                    p_low = p.astype(BF16)
                    p_ref[part, :] = p_low
                    out_t = out_t + nn(vt_ref[feats, pl.ds(columns[j], CHUNK)], p_low)
                out_t = out_t.astype(BF16).astype(F32)
                row_dot = jnp.sum(out_t * ubdt_ref[n], axis=0, keepdims=True)
                fold(att_parts, n, out_t.T)
                gq_t = jnp.zeros((256, 256), F32)
                for j in range(3):
                    part = pl.ds(CHUNK * j, CHUNK)
                    rows = pl.ds(starts[j], CHUNK)
                    grad_p = nt(v_ref[rows, feats], ubd_ref[n])
                    ds = (s_ref[part, :] * (grad_p - row_dot)).astype(BF16)
                    gv_ref[rows, feats] += nn(p_ref[part, :], ubd_ref[n])
                    gk_ref[rows, feats] += nn(ds, qbd_ref[n])
                    gq_t = gq_t + nn(kt_ref[feats, pl.ds(columns[j], CHUNK)], ds)
                fold(gq_parts, n, gq_t.T)

            for parts, ref, factor in ((att_parts, att_ref, 1.0), (gq_parts, gq_ref, 0.125)):
                ref[groups, 8 * c : 8 * c + 8, :] = jnp.zeros((12, 8, D), F32)
                for begin, end, n, piece in parts:
                    view = (
                        pl.ds(12 * r + begin // 8, (end - begin) // 8),
                        slice(8 * c, 8 * c + 8),
                        slice(128 * n, 128 * n + 256),
                    )
                    ref[view] += (piece * factor).reshape((end - begin) // 8, 8, 256)
        return carry

    lax.fori_loop(0, 4, latitude_band, 0)

    gq_low = gq_ref[...].reshape(768, D).astype(BF16)
    att_low = att_ref[...].reshape(768, D).astype(BF16)
    gwq_ref[...] = tn(tok_ref[own_rows, :], gq_low)
    gwo_ref[...] = tn(att_low, grad_ref[...])
    gwk_ref[...] = jnp.zeros((D, D), F32)
    gwv_ref[...] = jnp.zeros((D, D), F32)

    def finish(i, carry):
        rows = pl.ds(pl.multiple_of(i * 192, 192), 192)
        gk_low = gk_ref[rows, :].astype(BF16)
        gv_low = gv_ref[rows, :].astype(BF16)
        k_ref[rows, :] = gk_low
        v_ref[rows, :] = gv_low
        gk_ref[rows, :] = nt(gk_low, wk_ref[...]) + nt(gv_low, wv_ref[...])
        return carry

    lax.fori_loop(0, ALL // 192, finish, 0)
    for i in range(7):
        rows = pl.ds(384 * i, 384)
        x = tok_ref[rows, :]
        gwk_ref[...] += tn(x, k_ref[rows, :])
        gwv_ref[...] += tn(x, v_ref[rows, :])
    gt_own_ref[...] = gk_ref[own_rows, :] + nt(gq_low, wq_ref[...])
    gt_wide_ref[...] = gk_ref[...].astype(BF16)


def attention(row0, tok_wide, grad_out, w_query, w_key, w_value, w_out, lat_total):
    vmem = pl.BlockSpec(memory_space=pltpu.VMEM)
    weight = jax.ShapeDtypeStruct((D, D), F32)
    return pl.pallas_call(
        functools.partial(attention_kernel, lat_total),
        out_shape=(
            jax.ShapeDtypeStruct((768, D), F32),
            jax.ShapeDtypeStruct((ALL, D), BF16),
            weight,
            weight,
            weight,
            weight,
        ),
        in_specs=[pl.BlockSpec(memory_space=pltpu.SMEM)] + [vmem] * 6,
        out_specs=(vmem,) * 6,
        scratch_shapes=[
            pltpu.VMEM((ALL, D), BF16),
            pltpu.VMEM((ALL, D), BF16),
            pltpu.VMEM((D, 1536), BF16),
            pltpu.VMEM((D, 1536), BF16),
            pltpu.VMEM((48, 16, D), F32),
            pltpu.VMEM((48, 16, D), F32),
            pltpu.VMEM((ALL, D), F32),
            pltpu.VMEM((ALL, D), F32),
            pltpu.VMEM((48, 16, D), F32),
            pltpu.VMEM((48, 16, D), F32),
            pltpu.VMEM((3, 256, 256), BF16),
            pltpu.VMEM((3, 256, 256), BF16),
            pltpu.VMEM((3, 256, 256), F32),
            pltpu.VMEM((KEYS, 512), F32),
            pltpu.VMEM((KEYS, 256), F32),
            pltpu.VMEM((KEYS, 256), BF16),
        ],
        compiler_params=pltpu.CompilerParams(vmem_limit_bytes=56 * 1024 * 1024),
    )(row0, tok_wide, grad_out, w_query, w_key, w_value, w_out)


def shift(x, axis, step, closed):
    count = lax.axis_size(axis)
    pairs = [(i, (i + step) % count) for i in range(count) if closed or 0 <= i + step < count]
    return lax.ppermute(x, axis, pairs)


def on_device(tokens, w_query, w_key, w_value, w_out, grad_out):
    lat_dev = tokens.shape[0]
    lat_total = lat_dev * lax.axis_size("lat")
    x = tokens.transpose(0, 2, 1, 3)
    g = grad_out.transpose(0, 2, 1, 3).reshape(768, D)
    row0 = (lax.axis_index("lat") * lat_dev).astype(jnp.int32).reshape(1)

    above = shift(x[lat_dev - RIM :], "lat", 1, False)
    below = shift(x[:RIM], "lat", -1, False)
    strip = jnp.concatenate([above, x, below], axis=0)
    left = shift(strip[:, :, 8:], "lon", 1, True)
    right = shift(strip[:, :, :8], "lon", -1, True)
    wide = jnp.concatenate(
        [strip.reshape(OWN, D), left.reshape(SIDE, D), right.reshape(SIDE, D)], axis=0
    )

    gt_own, gt_wide, gwq, gwk, gwv, gwo = attention(
        row0, wide, g, w_query, w_key, w_value, w_out, lat_total
    )

    gwq, gwk, gwv, gwo = lax.psum((gwq, gwk, gwv, gwo), ("lat", "lon"))

    strip = gt_wide[:OWN].reshape(28, 3, 16, D)
    from_right = shift(gt_wide[OWN : OWN + SIDE].reshape(28, 3, 8, D), "lon", -1, True)
    from_left = shift(gt_wide[OWN + SIDE :].reshape(28, 3, 8, D), "lon", 1, True)
    add = jnp.concatenate([from_left, from_right], axis=2).astype(F32)
    edge_up = (strip[:RIM].astype(F32) + add[:RIM]).astype(BF16)
    edge_down = (strip[RIM + lat_dev :].astype(F32) + add[RIM + lat_dev :]).astype(BF16)
    to_up = shift(edge_up, "lat", -1, False).astype(F32)
    to_down = shift(edge_down, "lat", 1, False).astype(F32)
    total = gt_own.reshape(16, 3, 16, D) + add[RIM : RIM + lat_dev]
    middle = jnp.zeros((lat_dev - 2 * RIM, 3, 16, D), F32)
    total = total + jnp.concatenate([to_down, middle, to_up], axis=0)
    grad_tokens = total.astype(BF16).transpose(0, 2, 1, 3)
    return grad_tokens, gwq, gwk, gwv, gwo


def solution(mesh):
    placed = (P("lat", "lon", None, None), P(), P(), P(), P(), P("lat", "lon", None, None))
    return jax.shard_map(
        on_device,
        mesh=mesh,
        in_specs=placed,
        out_specs=(P("lat", "lon", None, None), P(), P(), P(), P()),
        check_vma=False,
    )
```

time: 879 us -> 297 us (0.34); the launches traced: 865 us -> 297 us
  local copies, waits for them, and re-layouts: 428 us -> 9.76 us
  matrix products: 99.2 us -> 0 us
  Pallas kernels: 0 us -> 74.1 us
  waiting for transfers between devices: 236 us -> 176 us
  other arithmetic: 55.8 us -> 5.17 us
  loops' own time: 16.5 us -> 0 us
    dynamic_update_slice x16 -> x0, local copies, waits for them, and re-layouts: 140 us -> none  [the longest x8 130 us: one_tile(): lax.dynamic_update_slice(extra_all, previous + grad_kv.reshape(tile_span,...]
    pallas_call x0 -> x1, Pallas kernels: none -> 74.1 us  [attention(): pl.pallas_call(functools.partial(attention_kernel, lat_total), out_shape=...]
    dot_general x31 -> x0, matrix products: 71 us -> none  [the longest x4 16.5 us: tile_grad(): jnp.einsum('qhd,khd->hqk', g_heads, v_heads, preferred_element_type=jnp.f...]
    reshape x37 -> x0, local copies, waits for them, and re-layouts: 56.6 us -> none  [the longest x4 24.4 us: one_tile(): kv_tile = lax.dynamic_slice(keyvals, starts, (tile_span, tile_span, level...]
    concatenate x10 -> x1, local copies, waits for them, and re-layouts: 53.5 us -> 0.07 us  [on_device(): total = total + jnp.concatenate([to_down, middle, to_up], axis=0)]
    ppermute x8, waiting for transfers between devices: 84.7 us -> 42.3 us  [shift(): return lax.ppermute(x, axis, pairs)]
    dynamic_slice x12 -> x0, local copies, waits for them, and re-layouts: 42.1 us -> none  [the longest x4 21.1 us: one_tile(): lax.dynamic_slice(keyvals, starts, (tile_span, tile_span, levels, 2 * mod...]
    slice x27 -> x4, local copies, waits for them, and re-layouts: 39.4 us -> 1.39 us  [the longest x1 1.15 us: on_device(): above = shift(x[lat_dev - RIM:], 'lat', 1, False)]
  transfers between devices with their start and end apart: 9 -> 9, of which waited for: 8 -> 7; matrix products, arithmetic and copies ran while one was open for 6% -> 1% of each run, Pallas kernels for 0% -> 0%
where the time goes in v1:
time: 297 us
  waiting for transfers between devices  176 us (59%)
  Pallas kernels  74.1 us (25%)
  starting transfers between devices  17.5 us (6%)
  between operations  14.2 us (5%)
  local copies, waits for them, and re-layouts  9.76 us (3%)
  other arithmetic  5.17 us (2%)
    psum x1, waiting for transfers between devices, on_device(): gwq, gwk, gwv, gwo = lax.psum((gwq, gwk, gwv, gwo), ('lat', 'lon'))  134 us
    pallas_call x1, Pallas kernels, attention(): pl.pallas_call(functools.partial(attention_kernel, lat_total), out_shape=...  74.1 us
    ppermute x8, waiting for transfers between devices, shift(): return lax.ppermute(x, axis, pairs)  42.3 us
    ppermute x8, starting transfers between devices, shift(): return lax.ppermute(x, axis, pairs)  17.5 us
    unnamed x16, local copies, waits for them, and re-layouts  8.29 us
  transfers between devices with their start and end apart: 9, of which 7 were waited for; matrix products, arithmetic and copies ran while one was open for 1% of the time, Pallas kernels for 0%

profile of v1, /device:TPU:1, one launch (start us, length us, event | category | flops | bytes accessed | tf_op | source)
XLA Modules:
  0.0 296.5 jit_solution(504730814787287370)
XLA Ops:
  7.2 1.2 fusion.8
  8.4 1.3 collective-permute-start.1
  9.7 5.0 %collective-permute-start = (bf16[6,3,16,512]{3,2,1,0:T(8,128)(2,1)S(1)}, bf16[6,3,16,512]{3,2,1,0:T(8,128)(2,1)S(1)}, u32[]{:S(2)}, u32[]{:S(2)}) collective-permute-start(bf16[6,3,16,512]{3,2,1,0:T(8,128)(2,1)S(1)} %get-tuple-element.29), channel_id=1, source_target_pairs={{0,16},{16,32},{32,48},{48,64},{64,80},{80,96},{96,112},{1,17},{17... | collective-permute-start | bytes 884744 | tf_op jit(solution)/shard_map/ppermute | solution.py:281
  14.7 4.8 %collective-permute-done.1 = bf16[6,3,16,512]{3,2,1,0:T(8,128)(2,1)S(1)} collective-permute-done((bf16[6,3,16,512]{3,2,1,0:T(8,128)(2,1)S(1)}, bf16[6,3,16,512]{3,2,1,0:T(8,128)(2,1)S(1)}, u32[]{:S(2)}, u32[]{:S(2)}) %collective-permute-start.1) | collective-permute-done | bytes 294944 | tf_op jit(solution)/shard_map/ppermute | solution.py:281
  19.5 0.9 collective-permute-done
  20.3 0.2 pad_maximum_fusion.1
  20.5 0.1 fusion.7
  20.6 1.6 collective-permute-start.3
  22.2 1.3 collective-permute-start.2
  23.5 15.9 %collective-permute-done.3 = bf16[28,3,8,512]{3,2,1,0:T(8,128)(2,1)S(1)} collective-permute-done((bf16[28,3,8,512]{3,2,1,0:T(8,128)(2,1)S(1)}, bf16[28,3,8,512]{3,2,1,0:T(8,128)(2,1)S(1)}, u32[]{:S(2)}, u32[]{:S(2)}) %collective-permute-start.3) | collective-permute-done | bytes 688160 | tf_op jit(solution)/shard_map/ppermute | solution.py:281
  39.4 2.8 pad_maximum_fusion.tok_ref
  42.3 74.1 %shard_map.101 = (f32[768,512]{1,0:T(8,128)}, bf16[2688,512]{1,0:T(8,128)(2,1)}, f32[512,512]{1,0:T(8,128)}, f32[512,512]{1,0:T(8,128)}, f32[512,512]{1,0:T(8,128)}, /*index=5*/f32[512,512]{1,0:T(8,128)}) custom-call(s32[1]{0:T(128)} %bitcast.row0_ref, bf16[2688,512]{1,0:T(8,128)(2,1)} %pad_maximum_fusion.tok_ref, bf16[768,512]{1,0:T(8,128)(2,1)} %bitcast.23, ...), custom_call_target="tpu_custom_call" | custom-call | tf_op jit(solution)/shard_map/pallas_call | solution.py:244
  116.4 1.8 copy-done.2
  118.1 0.1 fusion.6
  118.2 0.1 collective-permute-start.5
  118.3 1.8 collective-permute-start.4
  120.2 16.9 %collective-permute-done.5 = bf16[28,3,8,512]{3,2,1,0:T(8,128)(2,1)S(1)} collective-permute-done((bf16[28,3,8,512]{3,2,1,0:T(8,128)(2,1)S(1)}, bf16[28,3,8,512]{3,2,1,0:T(8,128)(2,1)S(1)}, u32[]{:S(2)}, u32[]{:S(2)}) %collective-permute-start.5) | collective-permute-done | bytes 688160 | tf_op jit(solution)/shard_map/ppermute | solution.py:281
  137.1 0.2 fusion.4
  137.3 1.3 collective-permute-start.7
  138.6 5.1 %collective-permute-start.6 = (bf16[6,3,16,512]{3,2,1,0:T(8,128)(2,1)S(1)}, bf16[6,3,16,512]{3,2,1,0:T(8,128)(2,1)S(1)}, u32[]{:S(2)}, u32[]{:S(2)}) collective-permute-start(bf16[6,3,16,512]{3,2,1,0:T(8,128)(2,1)S(1)} %get-tuple-element.25), channel_id=1, source_target_pairs={{0,16},{16,32},{32,48},{48,64},{64,80},{80,96},{96,112},{1,17},{17... | collective-permute-start | bytes 884744 | tf_op jit(solution)/shard_map/ppermute | solution.py:281
  143.7 0.1 pad.1.clone
  143.7 0.4 maximum_convert_fusion
  144.1 2.8 collective-permute-done.7
  147.0 1.0 collective-permute-done.6
  148.1 1.5 fusion.2
  149.6 133.6 %all-reduce.3.cloned.1.call-done = (f32[512,512]{1,0:T(8,128)}, f32[512,512]{1,0:T(8,128)}, f32[512,512]{1,0:T(8,128)}, f32[512,512]{1,0:T(8,128)}) async-done(((f32[512,512]{1,0:T(8,128)}, f32[512,512]{1,0:T(8,128)}, f32[512,512]{1,0:T(8,128)}, f32[512,512]{1,0:T(8,128)}), (f32[512,512]{1,0:T(8,128)}, f32[512,512]{1,0:T(8,128)}, f32[512,512]{1,0:T(8,128)}, ...) | async-done | bytes 4194320 | tf_op jit(solution)/shard_map/psum | solution.py:304
  283.1 2.4 copy.15
  285.5 1.0 copy.16
  286.5 0.6 copy-done.4
  287.1 1.0 copy.17
  288.1 0.6 copy-done.3
  288.7 1.0 copy.18
  (17 shorter events, 0.2 us)
Async XLA Ops:
  7.2 13.2 %copy-start = (bf16[16,16,3,512]{3,1,2,0:T(8,128)(2,1)S(1)}, bf16[16,16,3,512]{3,1,2,0:T(8,128)(2,1)}, u32[]{:S(2)}) copy-start(bf16[16,16,3,512]{3,1,2,0:T(8,128)(2,1)} %param.6) | copy-start | bytes 2359300
  7.2 276.0 %all-reduce.3.cloned.1.call-start = ((), (), s32[]{:S(2)}) async-start(), calls=%async_computation | async-start | bytes 8388608 | tf_op jit(solution)/shard_map/psum | solution.py:304
  8.4 11.1 %collective-permute-start.1 = (bf16[6,3,16,512]{3,2,1,0:T(8,128)(2,1)S(1)}, bf16[6,3,16,512]{3,2,1,0:T(8,128)(2,1)S(1)}, u32[]{:S(2)}, u32[]{:S(2)}) collective-permute-start(bf16[6,3,16,512]{3,2,1,0:T(8,128)(2,1)S(1)} %get-tuple-element.30), channel_id=1, source_target_pairs={{16,0},{32,16},{48,32},{64,48},{80,64},{96,80},{112,96},{17,1},{33... | collective-permute-start | bytes 884744 | tf_op jit(solution)/shard_map/ppermute | solution.py:281
  9.7 10.6 %collective-permute-start = (bf16[6,3,16,512]{3,2,1,0:T(8,128)(2,1)S(1)}, bf16[6,3,16,512]{3,2,1,0:T(8,128)(2,1)S(1)}, u32[]{:S(2)}, u32[]{:S(2)}) collective-permute-start(bf16[6,3,16,512]{3,2,1,0:T(8,128)(2,1)S(1)} %get-tuple-element.29), channel_id=1, source_target_pairs={{0,16},{16,32},{32,48},{48,64},{64,80},{80,96},{96,112},{1,17},{17... | collective-permute-start | bytes 884744 | tf_op jit(solution)/shard_map/ppermute | solution.py:281
  20.6 18.8 %collective-permute-start.3 = (bf16[28,3,8,512]{3,2,1,0:T(8,128)(2,1)S(1)}, bf16[28,3,8,512]{3,2,1,0:T(8,128)(2,1)S(1)}, u32[]{:S(2)}, u32[]{:S(2)}) collective-permute-start(bf16[28,3,8,512]{3,2,1,0:T(8,128)(2,1)S(1)} %get-tuple-element.28), channel_id=1, source_target_pairs={{0,15},{1,0},{2,1},{3,2},{4,3},{5,4},{6,5},{7,6},{8,7},{9,8},{10,9... | collective-permute-start | bytes 2064392 | tf_op jit(solution)/shard_map/ppermute | solution.py:281
  22.2 17.2 %collective-permute-start.2 = (bf16[28,3,8,512]{3,2,1,0:T(8,128)(2,1)S(1)}, bf16[28,3,8,512]{3,2,1,0:T(8,128)(2,1)}, u32[]{:S(2)}, u32[]{:S(2)}) collective-permute-start(bf16[28,3,8,512]{3,2,1,0:T(8,128)(2,1)S(1)} %get-tuple-element.27), channel_id=1, source_target_pairs={{0,1},{1,2},{2,3},{3,4},{4,5},{5,6},{6,7},{7,8},{8,9},{9,10},{10,1... | collective-permute-start | bytes 2064392 | tf_op jit(solution)/shard_map/ppermute | solution.py:281
  116.3 1.8 copy-start.2
  118.2 18.9 %collective-permute-start.5 = (bf16[28,3,8,512]{3,2,1,0:T(8,128)(2,1)S(1)}, bf16[28,3,8,512]{3,2,1,0:T(8,128)(2,1)S(1)}, u32[]{:S(2)}, u32[]{:S(2)}) collective-permute-start(bf16[28,3,8,512]{3,2,1,0:T(8,128)(2,1)S(1)} %bitcast.25), channel_id=1, source_target_pairs={{0,15},{1,0},{2,1},{3,2},{4,3},{5,4},{6,5},{7,6},{8,7},{9,8},{10,9... | collective-permute-start | bytes 2064392 | tf_op jit(solution)/shard_map/ppermute | solution.py:281
  118.3 18.8 %collective-permute-start.4 = (bf16[28,3,8,512]{3,2,1,0:T(8,128)(2,1)S(1)}, bf16[28,3,8,512]{3,2,1,0:T(8,128)(2,1)S(1)}, u32[]{:S(2)}, u32[]{:S(2)}) collective-permute-start(bf16[28,3,8,512]{3,2,1,0:T(8,128)(2,1)S(1)} %bitcast.24), channel_id=1, source_target_pairs={{0,1},{1,2},{2,3},{3,4},{4,5},{5,6},{6,7},{7,8},{8,9},{9,10},{10,1... | collective-permute-start | bytes 2064392 | tf_op jit(solution)/shard_map/ppermute | solution.py:281
  137.3 9.6 %collective-permute-start.7 = (bf16[6,3,16,512]{3,2,1,0:T(8,128)(2,1)S(1)}, bf16[6,3,16,512]{3,2,1,0:T(8,128)(2,1)S(1)}, u32[]{:S(2)}, u32[]{:S(2)}) collective-permute-start(bf16[6,3,16,512]{3,2,1,0:T(8,128)(2,1)S(1)} %get-tuple-element.26), channel_id=1, source_target_pairs={{16,0},{32,16},{48,32},{64,48},{80,64},{96,80},{112,96},{17,1},{33... | collective-permute-start | bytes 884744 | tf_op jit(solution)/shard_map/ppermute | solution.py:281
  138.6 9.4 %collective-permute-start.6 = (bf16[6,3,16,512]{3,2,1,0:T(8,128)(2,1)S(1)}, bf16[6,3,16,512]{3,2,1,0:T(8,128)(2,1)S(1)}, u32[]{:S(2)}, u32[]{:S(2)}) collective-permute-start(bf16[6,3,16,512]{3,2,1,0:T(8,128)(2,1)S(1)} %get-tuple-element.25), channel_id=1, source_target_pairs={{0,16},{16,32},{32,48},{48,64},{64,80},{80,96},{96,112},{1,17},{17... | collective-permute-start | bytes 884744 | tf_op jit(solution)/shard_map/ppermute | solution.py:281
  144.1 4.0 %copy-start.1 = (f32[768,512]{1,0:T(8,128)S(1)}, f32[768,512]{1,0:T(8,128)}, u32[]{:S(2)}) copy-start(f32[768,512]{1,0:T(8,128)} %get-tuple-element.11) | copy-start | bytes 4718596
  283.1 2.4 copy-start.5
  285.5 1.6 copy-start.4
  287.1 1.6 copy-start.3
Sparse Core Ops, SparseCore 0:
  116.5 166.5 all-reduce.2

commit v2 on v1

--- a/solution.py
+++ b/solution.py
@@ -18,6 +18,9 @@
 TQ = 96
 KEYS = 768 + 384
 CHUNK = 384
+PARTS = 4
+WIDTH = D // PARTS
+MESH = pl.DeviceIdType.MESH
 F32 = jnp.float32
 BF16 = jnp.bfloat16
 
@@ -45,10 +48,7 @@
     wo_ref,
     gt_own_ref,
     gt_wide_ref,
-    gwq_ref,
-    gwk_ref,
-    gwv_ref,
-    gwo_ref,
+    gw_ref,
     k_ref,
     v_ref,
     kt_ref,
@@ -214,10 +214,14 @@
 
     gq_low = gq_ref[...].reshape(768, D).astype(BF16)
     att_low = att_ref[...].reshape(768, D).astype(BF16)
-    gwq_ref[...] = tn(tok_ref[own_rows, :], gq_low)
-    gwo_ref[...] = tn(att_low, grad_ref[...])
-    gwk_ref[...] = jnp.zeros((D, D), F32)
-    gwv_ref[...] = jnp.zeros((D, D), F32)
+
+    def put(index, value):
+        for part in range(PARTS):
+            columns = value[:, WIDTH * part : WIDTH * part + WIDTH]
+            gw_ref[part, pl.ds(D * index, D), :] = columns.astype(BF16)
+
+    put(0, tn(tok_ref[own_rows, :], gq_low))
+    put(3, tn(att_low, grad_ref[...]))
 
     def finish(i, carry):
         rows = pl.ds(pl.multiple_of(i * 192, 192), 192)
@@ -229,30 +233,23 @@
         return carry
 
     lax.fori_loop(0, ALL // 192, finish, 0)
-    for i in range(7):
-        rows = pl.ds(384 * i, 384)
-        x = tok_ref[rows, :]
-        gwk_ref[...] += tn(x, k_ref[rows, :])
-        gwv_ref[...] += tn(x, v_ref[rows, :])
+    put(1, tn(tok_ref[...], k_ref[...]))
+    put(2, tn(tok_ref[...], v_ref[...]))
     gt_own_ref[...] = gk_ref[own_rows, :] + nt(gq_low, wq_ref[...])
     gt_wide_ref[...] = gk_ref[...].astype(BF16)
 
 
 def attention(row0, tok_wide, grad_out, w_query, w_key, w_value, w_out, lat_total):
     vmem = pl.BlockSpec(memory_space=pltpu.VMEM)
-    weight = jax.ShapeDtypeStruct((D, D), F32)
     return pl.pallas_call(
         functools.partial(attention_kernel, lat_total),
         out_shape=(
             jax.ShapeDtypeStruct((768, D), F32),
             jax.ShapeDtypeStruct((ALL, D), BF16),
-            weight,
-            weight,
-            weight,
-            weight,
+            jax.ShapeDtypeStruct((PARTS, 4 * D, WIDTH), BF16),
         ),
         in_specs=[pl.BlockSpec(memory_space=pltpu.SMEM)] + [vmem] * 6,
-        out_specs=(vmem,) * 6,
+        out_specs=(vmem,) * 3,
         scratch_shapes=[
             pltpu.VMEM((ALL, D), BF16),
             pltpu.VMEM((ALL, D), BF16),
@@ -275,47 +272,361 @@
     )(row0, tok_wide, grad_out, w_query, w_key, w_value, w_out)
 
 
-def shift(x, axis, step, closed):
-    count = lax.axis_size(axis)
-    pairs = [(i, (i + step) % count) for i in range(count) if closed or 0 <= i + step < count]
-    return lax.ppermute(x, axis, pairs)
+class Place:
+    def __init__(self):
+        self.lat = lax.axis_index("lat")
+        self.lon = lax.axis_index("lon")
+        self.z = self.lat % 4
+        self.core = self.lon % 2
+        self.x = self.lon // 4
+        self.y = (self.lat // 4) * 2 + (self.lon // 2) % 2
+        self.inside = {-1: self.lat > 0, 0: None, 1: self.lat < 7}
+
+    def near(self, dlat, dlon):
+        return (self.lat + dlat, lax.rem(self.lon + dlon + 16, 16))
+
+    def along(self, axis, step):
+        x, y, z = self.x, self.y, self.z
+        if axis == "x":
+            x = lax.rem(x + step, 4)
+        elif axis == "y":
+            y = lax.rem(y + step, 4)
+        else:
+            z = lax.rem(z + step, 4)
+        return ((y // 2) * 4 + z, x * 4 + (y % 2) * 2 + self.core)
+
+    def other_core(self):
+        return (self.lat, self.lon + 1 - 2 * self.core)
+
+    def index(self, axis):
+        return {"x": self.x, "y": self.y, "z": self.z}[axis]
+
+
+def guarded(condition, action):
+    if condition is None:
+        action()
+    else:
+        pl.when(condition)(action)
+
+
+def halo_copies(place, send_sem, recv_sem, routes):
+    copies = []
+    for i, (dlat, dlon, source, target) in enumerate(routes):
+        copy = pltpu.make_async_remote_copy(
+            src_ref=source,
+            dst_ref=target,
+            send_sem=send_sem.at[i],
+            recv_sem=recv_sem.at[i],
+            device_id=place.near(dlat, dlon),
+            device_id_type=MESH,
+        )
+        copies.append((place.inside[dlat], place.inside[-dlat], copy))
+    return copies
+
+
+def greet(place):
+    barrier = pltpu.get_barrier_semaphore()
+    for dlat in (-1, 0, 1):
+        for dlon in (-1, 0, 1):
+            if dlat or dlon:
+
+                def signal(dlat=dlat, dlon=dlon):
+                    pl.semaphore_signal(
+                        barrier, inc=1, device_id=place.near(dlat, dlon), device_id_type=MESH
+                    )
+
+                guarded(place.inside[dlat], signal)
+    rows = jnp.where(place.lat > 0, 3, 0) + jnp.where(place.lat < 7, 3, 0)
+    return barrier, 2 + rows
+
+
+def gather_kernel(x_ref, wide_ref, half_ref, send_sem, recv_sem):
+    place = Place()
+    barrier, count = greet(place)
+    x = x_ref[...].astype(F32).reshape(48, 16, D)
+    half_ref[0:384, :] = x[:, 0:8].reshape(384, D).astype(BF16)
+    half_ref[384:768, :] = x[:, 8:16].reshape(384, D).astype(BF16)
+    pl.semaphore_wait(barrier, count)
+
+    strip_first = {-1: 22, 0: 6, 1: 0}
+    rows = {-1: (0, 6), 0: (0, 16), 1: (10, 6)}
+    routes = []
+    for dlat in (-1, 0, 1):
+        begin, count = rows[dlat]
+        for dlon in (-1, 0, 1):
+            first = strip_first[dlat]
+            if dlon == 0:
+                if dlat == 0:
+                    continue
+                source = x_ref.at[pl.ds(48 * begin, 48 * count)]
+                target = wide_ref.at[pl.ds(48 * first, 48 * count)]
+            else:
+                half = 384 if dlon == 1 else 0
+                side = OWN if dlon == 1 else OWN + SIDE
+                source = half_ref.at[pl.ds(half + 24 * begin, 24 * count)]
+                target = wide_ref.at[pl.ds(side + 24 * first, 24 * count)]
+            routes.append((dlat, dlon, source, target))
+    copies = halo_copies(place, send_sem, recv_sem, routes)
+    for sends, _, copy in copies:
+        guarded(sends, copy.start)
+    wide_ref[pl.ds(RIM * 48, 768), :] = x_ref[...]
+
+    def clear(first):
+        wide_ref[pl.ds(48 * first, 288), :] = jnp.zeros((288, D), BF16)
+        wide_ref[pl.ds(OWN + 24 * first, 144), :] = jnp.zeros((144, D), BF16)
+        wide_ref[pl.ds(OWN + SIDE + 24 * first, 144), :] = jnp.zeros((144, D), BF16)
+
+    pl.when(place.lat == 0)(lambda: clear(0))
+    pl.when(place.lat == 7)(lambda: clear(22))
+    for sends, receives, copy in copies:
+        guarded(sends, copy.wait_send)
+        guarded(receives, copy.wait_recv)
+
+
+def gather(x):
+    vmem = pl.BlockSpec(memory_space=pltpu.VMEM)
+    return pl.pallas_call(
+        gather_kernel,
+        out_shape=jax.ShapeDtypeStruct((ALL, D), BF16),
+        in_specs=[vmem],
+        out_specs=vmem,
+        scratch_shapes=[
+            pltpu.VMEM((768, D), BF16),
+            pltpu.SemaphoreType.DMA((8,)),
+            pltpu.SemaphoreType.DMA((8,)),
+        ],
+        compiler_params=pltpu.CompilerParams(
+            collective_id=0, has_side_effects=True, vmem_limit_bytes=24 * 1024 * 1024
+        ),
+    )(x)
+
+
+ORDERS = (("x", "y", "z"), ("y", "z", "x"), ("z", "x", "y"), ("x", "z", "y"))
+BLOCKS = (256, 64, 16)
+
+
+def reduce_kernel(
+    own_ref,
+    wide_ref,
+    gw_ref,
+    out_ref,
+    sum_ref,
+    middle_ref,
+    sides_ref,
+    acc_ref,
+    pair_ref,
+    send0,
+    recv0,
+    send1,
+    recv1,
+    send2,
+    recv2,
+    halo_send,
+    halo_recv,
+    pair_send,
+    pair_recv,
+    ring_send,
+    ring_recv,
+    back_send,
+    back_recv,
+    last_send,
+    last_recv,
+):
+    place = Place()
+    barrier, count = greet(place)
+    partners = [place.other_core()]
+    partners += [place.along(axis, step) for axis in "xyz" for step in (1, 2, 3)]
+    for partner in partners:
+        pl.semaphore_signal(barrier, inc=1, device_id=partner, device_id_type=MESH)
+    pl.semaphore_wait(barrier, count + len(partners))
+
+    mine = pl.multiple_of(place.core * 1024, 1024)
+    theirs = pl.multiple_of(1024 - place.core * 1024, 1024)
+    waits = []
+
+    def send(source, target, send_sem, recv_sem, device):
+        copy = pltpu.make_async_remote_copy(
+            src_ref=source,
+            dst_ref=target,
+            send_sem=send_sem,
+            recv_sem=recv_sem,
+            device_id=device,
+            device_id_type=MESH,
+        )
+        copy.start()
+        waits.append(copy)
+        return copy
+
+    pair = [
+        send(
+            gw_ref.at[p, pl.ds(theirs, 1024)],
+            pair_ref.at[p],
+            pair_send.at[p],
+            pair_recv.at[p],
+            place.other_core(),
+        )
+        for p in range(PARTS)
+    ]
+
+    strip_first = {-1: 0, 0: 6, 1: 22}
+    middle_slot = {-1: 0, 1: 288}
+    side_slot = {-1: 0, 0: 144, 1: 528}
+    routes = []
+    for dlat in (-1, 0, 1):
+        rows = 16 if dlat == 0 else 6
+        for dlon in (-1, 0, 1):
+            first = strip_first[dlat]
+            if dlon == 0:
+                if dlat == 0:
+                    continue
+                source = wide_ref.at[pl.ds(48 * first, 48 * rows)]
+                target = middle_ref.at[pl.ds(middle_slot[dlat], 48 * rows)]
+            else:
+                side = OWN if dlon == -1 else OWN + SIDE
+                slot = SIDE if dlon == -1 else 0
+                source = wide_ref.at[pl.ds(side + 24 * first, 24 * rows)]
+                target = sides_ref.at[pl.ds(slot + side_slot[dlat], 24 * rows)]
+            routes.append((dlat, dlon, source, target))
+    halo = halo_copies(place, halo_send, halo_recv, routes)
+    for sends, _, copy in halo:
+        guarded(sends, copy.start)
+
+    buffers = ((send0, recv0), (send1, recv1), (send2, recv2))
+    pending = [[pair[p]] for p in range(PARTS)]
+    base = [0] * PARTS
+    for stage in range(3):
+        rows = BLOCKS[stage]
+        outgoing, incoming = buffers[stage]
+        for p in range(PARTS):
+            for copy in pending[p]:
+                copy.wait_recv()
+            if stage == 0:
+                acc_ref[p] = gw_ref[p, pl.ds(mine, 1024), :].astype(F32) + pair_ref[p].astype(F32)
+            else:
+                before = buffers[stage - 1][1]
+                here = pl.ds(base[p], BLOCKS[stage - 1])
+                total = acc_ref[p, here, :]
+                for step in range(3):
+                    total = total + before[p, step].astype(F32)
+                acc_ref[p, here, :] = total
+            axis = ORDERS[p][stage]
+            me = place.index(axis)
+            pending[p] = []
+            for step in (1, 2, 3):
+                block = base[p] + lax.rem(me + step, 4) * rows
+                block = pl.multiple_of(block, rows)
+                outgoing[p, step - 1] = acc_ref[p, pl.ds(block, rows), :].astype(BF16)
+                slot = (p * 3 + stage) * 3 + step - 1
+                pending[p].append(
+                    send(
+                        outgoing.at[p, step - 1],
+                        incoming.at[p, step - 1],
+                        ring_send.at[slot],
+                        ring_recv.at[slot],
+                        place.along(axis, step),
+                    )
+                )
+            base[p] = pl.multiple_of(base[p] + me * rows, rows)
+
+    for stage in (3, 2, 1, 0):
+        for p in range(PARTS):
+            for copy in pending[p]:
+                copy.wait_recv()
+            if stage == 3:
+                here = pl.ds(base[p], 16)
+                total = acc_ref[p, here, :]
+                for step in range(3):
+                    total = total + recv2[p, step].astype(F32)
+                sum_ref[p, pl.ds(pl.multiple_of(mine + base[p], 16), 16), :] = total.astype(BF16)
+            if stage > 0:
+                rows = BLOCKS[stage - 1]
+                axis = ORDERS[p][stage - 1]
+                here = sum_ref.at[p, pl.ds(pl.multiple_of(mine + base[p], rows), rows)]
+                pending[p] = []
+                for step in (1, 2, 3):
+                    slot = (p * 3 + stage - 1) * 3 + step - 1
+                    pending[p].append(
+                        send(
+                            here,
+                            here,
+                            back_send.at[slot],
+                            back_recv.at[slot],
+                            place.along(axis, step),
+                        )
+                    )
+                base[p] = base[p] - place.index(axis) * rows
+            else:
+                here = sum_ref.at[p, pl.ds(mine, 1024)]
+                pending[p] = [
+                    send(here, here, last_send.at[p], last_recv.at[p], place.other_core())
+                ]
+
+    for sends, receives, copy in halo:
+        guarded(sends, copy.wait_send)
+        guarded(receives, copy.wait_recv)
+    for half in range(2):
+        part = sides_ref[pl.ds(SIDE * half + 144, 384), :].astype(F32).reshape(48, 8, D)
+        own_ref_part = own_ref[:, 8 * half : 8 * half + 8, :]
+        acc = own_ref_part + part
+        out_ref[:, 8 * half : 8 * half + 8, :] = acc
+
+    def edge(slot, side, first):
+        rows = pl.ds(3 * first, 18)
+        out_ref[rows] = out_ref[rows] + middle_ref[pl.ds(slot, 288), :].astype(F32).reshape(18, 16, D)
+        for half in range(2):
+            part = sides_ref[pl.ds(SIDE * half + side, 144), :].astype(F32).reshape(18, 8, D)
+            view = out_ref[rows, 8 * half : 8 * half + 8, :]
+            out_ref[rows, 8 * half : 8 * half + 8, :] = view + part
+
+    pl.when(place.lat < 7)(lambda: edge(0, 0, 10))
+    pl.when(place.lat > 0)(lambda: edge(288, 528, 0))
+
+    for p in range(PARTS):
+        pending[p][0].wait_recv()
+    for copy in waits:
+        copy.wait_send()
+
+
+def reduce(gt_own, gt_wide, gw):
+    vmem = pl.BlockSpec(memory_space=pltpu.VMEM)
+    dma = pltpu.SemaphoreType.DMA
+    scratch = [
+        pltpu.VMEM((576, D), BF16),
+        pltpu.VMEM((2 * SIDE, D), BF16),
+        pltpu.VMEM((PARTS, 1024, WIDTH), F32),
+        pltpu.VMEM((PARTS, 1024, WIDTH), BF16),
+    ]
+    for rows in BLOCKS:
+        scratch += [pltpu.VMEM((PARTS, 3, rows, WIDTH), BF16)] * 2
+    for count in (8, PARTS, 9 * PARTS, 9 * PARTS, PARTS):
+        scratch += [dma((count,))] * 2
+    return pl.pallas_call(
+        reduce_kernel,
+        out_shape=(
+            jax.ShapeDtypeStruct((48, 16, D), F32),
+            jax.ShapeDtypeStruct((PARTS, 4 * D, WIDTH), BF16),
+        ),
+        in_specs=[vmem] * 3,
+        out_specs=(vmem,) * 2,
+        scratch_shapes=scratch,
+        compiler_params=pltpu.CompilerParams(
+            collective_id=1, has_side_effects=True, vmem_limit_bytes=40 * 1024 * 1024
+        ),
+    )(gt_own.reshape(48, 16, D), gt_wide, gw)
 
 
 def on_device(tokens, w_query, w_key, w_value, w_out, grad_out):
     lat_dev = tokens.shape[0]
     lat_total = lat_dev * lax.axis_size("lat")
-    x = tokens.transpose(0, 2, 1, 3)
+    x = tokens.transpose(0, 2, 1, 3).reshape(768, D)
     g = grad_out.transpose(0, 2, 1, 3).reshape(768, D)
     row0 = (lax.axis_index("lat") * lat_dev).astype(jnp.int32).reshape(1)
-
-    above = shift(x[lat_dev - RIM :], "lat", 1, False)
-    below = shift(x[:RIM], "lat", -1, False)
-    strip = jnp.concatenate([above, x, below], axis=0)
-    left = shift(strip[:, :, 8:], "lon", 1, True)
-    right = shift(strip[:, :, :8], "lon", -1, True)
-    wide = jnp.concatenate(
-        [strip.reshape(OWN, D), left.reshape(SIDE, D), right.reshape(SIDE, D)], axis=0
-    )
-
-    gt_own, gt_wide, gwq, gwk, gwv, gwo = attention(
-        row0, wide, g, w_query, w_key, w_value, w_out, lat_total
-    )
-
-    gwq, gwk, gwv, gwo = lax.psum((gwq, gwk, gwv, gwo), ("lat", "lon"))
-
-    strip = gt_wide[:OWN].reshape(28, 3, 16, D)
-    from_right = shift(gt_wide[OWN : OWN + SIDE].reshape(28, 3, 8, D), "lon", -1, True)
-    from_left = shift(gt_wide[OWN + SIDE :].reshape(28, 3, 8, D), "lon", 1, True)
-    add = jnp.concatenate([from_left, from_right], axis=2).astype(F32)
-    edge_up = (strip[:RIM].astype(F32) + add[:RIM]).astype(BF16)
-    edge_down = (strip[RIM + lat_dev :].astype(F32) + add[RIM + lat_dev :]).astype(BF16)
-    to_up = shift(edge_up, "lat", -1, False).astype(F32)
-    to_down = shift(edge_down, "lat", 1, False).astype(F32)
-    total = gt_own.reshape(16, 3, 16, D) + add[RIM : RIM + lat_dev]
-    middle = jnp.zeros((lat_dev - 2 * RIM, 3, 16, D), F32)
-    total = total + jnp.concatenate([to_down, middle, to_up], axis=0)
-    grad_tokens = total.astype(BF16).transpose(0, 2, 1, 3)
-    return grad_tokens, gwq, gwk, gwv, gwo
+    wide = gather(x)
+    gt_own, gt_wide, gw = attention(row0, wide, g, w_query, w_key, w_value, w_out, lat_total)
+    grad_tokens, sums = reduce(gt_own, gt_wide, gw)
+    grad_tokens = grad_tokens.reshape(16, 3, 16, D).transpose(0, 2, 1, 3).astype(BF16)
+    sums = sums.reshape(PARTS, 4, D, WIDTH).transpose(1, 2, 0, 3).reshape(4, D, D).astype(F32)
+    return grad_tokens, sums[0], sums[1], sums[2], sums[3]
 
 
 def solution(mesh):

time: 297 us -> 173 us (0.58)
  waiting for transfers between devices: 176 us -> 0 us
  Pallas kernels: 74.1 us -> 157 us
  starting transfers between devices: 17.5 us -> 0 us
  between operations: 14.2 us -> 0.71 us
  other arithmetic: 5.17 us -> 1.42 us
  local copies, waits for them, and re-layouts: 9.76 us -> 13.5 us
    psum x1 -> x0, waiting for transfers between devices: 134 us -> none  [on_device(): gwq, gwk, gwv, gwo = lax.psum((gwq, gwk, gwv, gwo), ('lat', 'lon'))]
    pallas_call x0 -> x2, Pallas kernels: none -> 83.8 us  [the longest x1 64.4 us: reduce(): pl.pallas_call(reduce_kernel, out_shape=(jax.ShapeDtypeStruct((48, 16, D)...]
    ppermute x8 -> x0, waiting for transfers between devices: 42.3 us -> none  [shift(): return lax.ppermute(x, axis, pairs)]
    ppermute x8 -> x0, starting transfers between devices: 17.5 us -> none  [shift(): return lax.ppermute(x, axis, pairs)]
    concatenate x2 -> x0, other arithmetic: 3 us -> none  [the longest x1 2.84 us: on_device(): jnp.concatenate([strip.reshape(OWN, D), left.reshape(SIDE, D), right.resh...]
    squeeze x0 -> x2, local copies, waits for them, and re-layouts: none -> 2.97 us  [on_device(): return (grad_tokens, sums[0], sums[1], sums[2], sums[3])]
    unnamed x16 -> x10, local copies, waits for them, and re-layouts: 8.29 us -> 7.43 us
  transfers between devices with their start and end apart: 9 -> 0, of which waited for: 7 -> 0; matrix products, arithmetic and copies ran while one was open for 1% -> 0% of each run, Pallas kernels for 0% -> 0%
where the time goes in v2:
time: 173 us; the launch traced here: 172 us
  Pallas kernels  157 us (91%)
  local copies, waits for them, and re-layouts  13.5 us (8%)
    pallas_call x1, Pallas kernels, attention(): pl.pallas_call(functools.partial(attention_kernel, lat_total), out_shape=...  73 us
    pallas_call x1, Pallas kernels, reduce(): pl.pallas_call(reduce_kernel, out_shape=(jax.ShapeDtypeStruct((48, 16, D)...  64.4 us
    pallas_call x1, Pallas kernels, gather(): pl.pallas_call(gather_kernel, out_shape=jax.ShapeDtypeStruct((ALL, D), BF...  19.4 us
    unnamed x10, local copies, waits for them, and re-layouts  7.43 us

profile of v2, /device:TPU:1, one launch (start us, length us, event | category | flops | bytes accessed | tf_op | source)
XLA Modules:
  0.0 172.4 jit_solution(11299966905011985972)
XLA Ops:
  0.6 0.0 copy-start.4
  0.6 1.1 copy-done.4
  1.8 19.4 %shard_map.101.tok_ref = bf16[2688,512]{1,0:T(8,128)(2,1)S(1)} custom-call(bf16[768,512]{1,0:T(8,128)(2,1)S(1)} %bitcast.33), custom_call_target="tpu_custom_call" | custom-call | tf_op jit(solution)/shard_map/pallas_call | solution.py:388
  21.2 0.0 copy-start
  21.2 1.5 copy-done
  22.7 73.0 %shard_map.102 = (f32[768,512]{1,0:T(8,128)}, bf16[2688,512]{1,0:T(8,128)(2,1)}, bf16[4,2048,128]{2,1,0:T(8,128)(2,1)}) custom-call(s32[1]{0:T(128)} %bitcast.row0_ref, bf16[2688,512]{1,0:T(8,128)(2,1)} %copy-done, bf16[768,512]{1,0:T(8,128)(2,1)} %bitcast.39, bf16[512,512]{1,0:T(8,128)(2,1)} %wq_ref.1, bf16[512,512]{1,0:T(8,128)(2,1)} %wk_ref.1, ...), custom_call_target="tpu_custom_call" | custom-call | tf_op jit(solution)/shard_map/pallas_call | solution.py:244
  95.7 0.0 copy-start.1
  95.7 1.8 %copy-done.1 = bf16[2688,512]{1,0:T(8,128)(2,1)S(1)} copy-done((bf16[2688,512]{1,0:T(8,128)(2,1)S(1)}, bf16[2688,512]{1,0:T(8,128)(2,1)}, u32[]{:S(2)}) %copy-start.1) | copy-done | bytes 2752536
  97.5 0.0 copy-start.2
  97.5 1.6 copy-done.2
  99.1 0.0 copy-start.3
  99.1 1.4 copy-done.3
  100.5 64.4 %shard_map.103 = (f32[48,16,512]{2,1,0:T(8,128)S(1)}, bf16[4,2048,128]{2,1,0:T(8,128)(2,1)S(1)}) custom-call(f32[48,16,512]{2,1,0:T(8,128)S(1)} %bitcast.32, bf16[2688,512]{1,0:T(8,128)(2,1)S(1)} %copy-done.1, bf16[4,2048,128]{2,1,0:T(8,128)(2,1)S(1)} %copy-done.2), custom_call_target="tpu_custom_call" | custom-call | tf_op jit(solution)/shard_map/pallas_call | solution.py:603
  164.9 1.0 convert_element_type.19
  165.9 0.4 convert_bitcast_fusion
  166.3 0.4 fusion
  166.7 0.7 copy.14
  167.4 0.7 copy.13
  168.1 1.5 copy_bitcast_fusion
  169.5 0.7 copy.12
  170.2 0.7 copy.11
  170.9 1.5 copy_bitcast_fusion.2
Async XLA Ops:
  0.6 1.1 copy-start.4
  21.2 1.5 copy-start
  95.7 1.8 %copy-start.1 = (bf16[2688,512]{1,0:T(8,128)(2,1)S(1)}, bf16[2688,512]{1,0:T(8,128)(2,1)}, u32[]{:S(2)}) copy-start(bf16[2688,512]{1,0:T(8,128)(2,1)} %get-tuple-element.11.wide_ref) | copy-start | bytes 8257540
  97.5 1.6 copy-start.2
  99.1 1.4 copy-start.3

commit v3 on v2

--- a/solution.py
+++ b/solution.py
@@ -65,20 +65,21 @@
     bias_ref,
     s_ref,
     p_ref,
+    ds_ref,
 ):
     row0 = row0_ref[0]
     own_rows = pl.ds(RIM * 48, 768)
 
     def project(i, carry):
-        rows = pl.ds(pl.multiple_of(i * 192, 192), 192)
+        rows = pl.ds(pl.multiple_of(i * 672, 672), 672)
         x = tok_ref[rows, :]
         k_ref[rows, :] = nn(x, wk_ref[...]).astype(BF16)
         v_ref[rows, :] = nn(x, wv_ref[...]).astype(BF16)
-        gk_ref[rows, :] = jnp.zeros((192, D), F32)
-        gv_ref[rows, :] = jnp.zeros((192, D), F32)
+        gk_ref[rows, :] = jnp.zeros((672, D), F32)
+        gv_ref[rows, :] = jnp.zeros((672, D), F32)
         return carry
 
-    lax.fori_loop(0, ALL // 192, project, 0)
+    lax.fori_loop(0, ALL // 672, project, 0)
     for i in range(4):
         x = tok_ref[pl.ds(RIM * 48 + 192 * i, 192), :]
         q = nn(x, wq_ref[...]).astype(BF16).astype(F32) * 0.125
@@ -98,39 +99,32 @@
         lowest = jnp.where(row0 == 0, RIM, 0)
         highest = jnp.where(row0 + 16 == lat_total, RIM, 12)
         base = jnp.clip(4 * r, lowest, highest)
-        for i in range(2):
-            part = pl.ds(pl.multiple_of(base * 48 + 384 * i, 48), 384)
-            kt_ref[:, pl.ds(384 * i, 384)] = k_ref[part, :].T
-            vt_ref[:, pl.ds(384 * i, 384)] = v_ref[part, :].T
+        own = [pl.multiple_of(base * 48 + 384 * i, 48) for i in range(2)]
+        side = [pl.multiple_of(OWN + SIDE * c + base * 24, 48) for c in range(2)]
+        for i, start in enumerate((side[0], own[0], own[1], side[1])):
+            part = pl.ds(start, CHUNK)
+            kt_ref[:, pl.ds(CHUNK * i, CHUNK)] = k_ref[part, :].T
+            vt_ref[:, pl.ds(CHUNK * i, CHUNK)] = v_ref[part, :].T
+        starts = ((side[0], own[0], own[1]), (own[0], own[1], side[1]))
+        groups = pl.ds(12 * r, 12)
+
         for c in range(2):
-            part = pl.ds(pl.multiple_of(OWN + SIDE * c + base * 24, 48), 384)
-            kt_ref[:, pl.ds(768 + 384 * c, 384)] = k_ref[part, :].T
-            vt_ref[:, pl.ds(768 + 384 * c, 384)] = v_ref[part, :].T
-
-        for c in range(2):
-            starts = [
-                pl.multiple_of(base * 48, 48),
-                pl.multiple_of(base * 48 + 384, 48),
-                pl.multiple_of(OWN + SIDE * c + base * 24, 48),
-            ]
-            columns = [0, 384, 768 + 384 * c]
-
             lane = lax.broadcasted_iota(jnp.int32, (1, 512), 1) % TQ
             q_lat = row0 + 4 * r + lane // 24
             first = jnp.clip(q_lat - RIM, 0, lat_total - SPAN) - (row0 + base - RIM)
             q_col = lane % 8
+
+            def bias(d_lat, d_col):
+                inside = (d_lat >= 0) & (d_lat < SPAN) & (d_col >= 0) & (d_col < SPAN)
+                return jnp.where(inside, 0.0, -jnp.inf)
+
             key = lax.broadcasted_iota(jnp.int32, (768, 1), 0)
-            d_lat = key // 48 - first
-            d_col = key % 16 - 8 * c - q_col + RIM
-            inside = (d_lat >= 0) & (d_lat < SPAN) & (d_col >= 0) & (d_col < SPAN)
-            bias_ref[0:768, :] = jnp.where(inside, 0.0, -jnp.inf)
+            rows = pl.ds(CHUNK * (1 - c), 768)
+            bias_ref[c, rows, :] = bias(key // 48 - first, key % 16 - 8 * c - q_col + RIM)
             key = lax.broadcasted_iota(jnp.int32, (384, 1), 0)
-            d_lat = key // 24 - first
-            d_col = key % 8 + (16 * c - 8) - q_col + RIM
-            inside = (d_lat >= 0) & (d_lat < SPAN) & (d_col >= 0) & (d_col < SPAN)
-            bias_ref[768:1152, :] = jnp.where(inside, 0.0, -jnp.inf)
-
-            groups = pl.ds(12 * r, 12)
+            rows = pl.ds(768 * c, 384)
+            bias_ref[c, rows, :] = bias(key // 24 - first, key % 8 + (16 * c - 8) - q_col + RIM)
+
             q_tile = q_ref[groups, 8 * c : 8 * c + 8, :].reshape(TQ, D).astype(BF16)
             u_tile = u_ref[groups, 8 * c : 8 * c + 8, :].reshape(TQ, D).astype(BF16)
             q_all = jnp.concatenate([q_tile] * HEADS, axis=0)
@@ -138,81 +132,100 @@
             for n in range(3):
                 keep = diagonal(n)
                 block = q_all[256 * n : 256 * n + 256, 128 * n : 128 * n + 256]
-                qbd_ref[n] = jnp.where(keep, block, jnp.zeros_like(block))
+                qbd_ref[3 * c + n] = jnp.where(keep, block, jnp.zeros_like(block))
                 block = u_all[256 * n : 256 * n + 256, 128 * n : 128 * n + 256]
                 block = jnp.where(keep, block, jnp.zeros_like(block))
-                ubd_ref[n] = block
-                ubdt_ref[n] = block.astype(F32).T
-
-            att_parts = [None] * HEADS
-            gq_parts = [None] * HEADS
-
-            def fold(parts, n, block):
-                block = jnp.where(diagonal(n), block, 0.0)
-                row = 256 * n
-                while row < 256 * n + 256:
-                    h = row // TQ
-                    end = min(TQ * (h + 1), 256 * n + 256)
-                    piece = block[row - 256 * n : end - 256 * n]
-                    parts.append((row - TQ * h, end - TQ * h, n, piece))
-                    row = end
-
-            att_parts = []
-            gq_parts = []
-            for n in range(3):
-                feats = pl.ds(128 * n, 256)
-                bias_lane = (0, 256, 128)[n]
-                high = jnp.full((8, 256), -jnp.inf, F32)
-                for j in range(3):
-                    rows = pl.ds(starts[j], CHUNK)
-                    s = nt(k_ref[rows, feats], qbd_ref[n])
-                    s = s + bias_ref[pl.ds(CHUNK * j, CHUNK), pl.ds(bias_lane, 256)]
-                    s_ref[pl.ds(CHUNK * j, CHUNK), :] = s
-                    high = jnp.maximum(high, jnp.max(s.reshape(CHUNK // 8, 8, 256), axis=0))
-                high = jnp.max(high, axis=0, keepdims=True)
-                total = jnp.zeros((8, 256), F32)
-                for j in range(3):
-                    part = pl.ds(CHUNK * j, CHUNK)
-                    e = jnp.exp(s_ref[part, :] - high)
-                    s_ref[part, :] = e
-                    total = total + jnp.sum(e.reshape(CHUNK // 8, 8, 256), axis=0)
-                scale = 1.0 / jnp.sum(total, axis=0, keepdims=True)
-                out_t = jnp.zeros((256, 256), F32)
-                for j in range(3):
-                    part = pl.ds(CHUNK * j, CHUNK)
-                    p = s_ref[part, :] * scale
-                    s_ref[part, :] = p
-                    p_low = p.astype(BF16)
-                    p_ref[part, :] = p_low
-                    out_t = out_t + nn(vt_ref[feats, pl.ds(columns[j], CHUNK)], p_low)
-                out_t = out_t.astype(BF16).astype(F32)
-                row_dot = jnp.sum(out_t * ubdt_ref[n], axis=0, keepdims=True)
-                fold(att_parts, n, out_t.T)
-                gq_t = jnp.zeros((256, 256), F32)
-                for j in range(3):
-                    part = pl.ds(CHUNK * j, CHUNK)
-                    rows = pl.ds(starts[j], CHUNK)
-                    grad_p = nt(v_ref[rows, feats], ubd_ref[n])
-                    ds = (s_ref[part, :] * (grad_p - row_dot)).astype(BF16)
-                    gv_ref[rows, feats] += nn(p_ref[part, :], ubd_ref[n])
-                    gk_ref[rows, feats] += nn(ds, qbd_ref[n])
-                    gq_t = gq_t + nn(kt_ref[feats, pl.ds(columns[j], CHUNK)], ds)
-                fold(gq_parts, n, gq_t.T)
-
-            for parts, ref, factor in ((att_parts, att_ref, 1.0), (gq_parts, gq_ref, 0.125)):
-                ref[groups, 8 * c : 8 * c + 8, :] = jnp.zeros((12, 8, D), F32)
-                for begin, end, n, piece in parts:
-                    view = (
-                        pl.ds(12 * r + begin // 8, (end - begin) // 8),
-                        slice(8 * c, 8 * c + 8),
-                        slice(128 * n, 128 * n + 256),
-                    )
-                    ref[view] += (piece * factor).reshape((end - begin) // 8, 8, 256)
+                ubd_ref[3 * c + n] = block
+                ubdt_ref[3 * c + n] = block.astype(F32).T
+            att_ref[groups, 8 * c : 8 * c + 8, :] = jnp.zeros((12, 8, D), F32)
+            gq_ref[groups, 8 * c : 8 * c + 8, :] = jnp.zeros((12, 8, D), F32)
+
+        def fold(ref, c, n, block):
+            block = jnp.where(diagonal(n), block, 0.0)
+            row = 256 * n
+            while row < 256 * n + 256:
+                h = row // TQ
+                end = min(TQ * (h + 1), 256 * n + 256)
+                begin = row - TQ * h
+                count = (end - row) // 8
+                view = (
+                    pl.ds(12 * r + begin // 8, count),
+                    slice(8 * c, 8 * c + 8),
+                    slice(128 * n, 128 * n + 256),
+                )
+                ref[view] += block[row - 256 * n : end - 256 * n].reshape(count, 8, 256)
+                row = end
+
+        state = [{} for _ in range(6)]
+
+        def parts(b):
+            return b // 3, b % 3, pl.ds(128 * (b % 3), 256)
+
+        def score(b):
+            c, n, feats = parts(b)
+            bias_lane = pl.ds((0, 256, 128)[n], 256)
+            high = jnp.full((8, 256), -jnp.inf, F32)
+            for j in range(3):
+                part = pl.ds(CHUNK * j, CHUNK)
+                x = nt(k_ref[pl.ds(starts[c][j], CHUNK), feats], qbd_ref[b])
+                x = x + bias_ref[c, part, bias_lane]
+                s_ref[b, part, :] = x
+                high = jnp.maximum(high, jnp.max(x.reshape(CHUNK // 8, 8, 256), axis=0))
+                yield
+            state[b]["high"] = jnp.max(high, axis=0, keepdims=True)
+
+        def exponent(b):
+            high = state[b]["high"]
+            total = jnp.zeros((8, 256), F32)
+            for j in range(3):
+                part = pl.ds(CHUNK * j, CHUNK)
+                e = jnp.exp(s_ref[b, part, :] - high)
+                s_ref[b, part, :] = e
+                total = total + jnp.sum(e.reshape(CHUNK // 8, 8, 256), axis=0)
+                yield
+            state[b]["scale"] = 1.0 / jnp.sum(total, axis=0, keepdims=True)
+
+        def attend(b):
+            c, n, feats = parts(b)
+            scale = state[b]["scale"]
+            for j in range(3):
+                part = pl.ds(CHUNK * j, CHUNK)
+                p = s_ref[b, part, :] * scale
+                s_ref[b, part, :] = p
+                p_ref[b, part, :] = p.astype(BF16)
+                yield
+            out_t = nn(vt_ref[feats, pl.ds(CHUNK * c, KEYS)], p_ref[b])
+            out_t = out_t.astype(BF16).astype(F32)
+            state[b]["row_dot"] = jnp.sum(out_t * ubdt_ref[b], axis=0, keepdims=True)
+            fold(att_ref, c, n, out_t.T)
+
+        def gradient(b):
+            c, n, feats = parts(b)
+            row_dot = state[b]["row_dot"]
+            for j in range(3):
+                part = pl.ds(CHUNK * j, CHUNK)
+                rows = pl.ds(starts[c][j], CHUNK)
+                grad_p = nt(v_ref[rows, feats], ubd_ref[b])
+                ds = (s_ref[b, part, :] * (grad_p - row_dot)).astype(BF16)
+                ds_ref[b, part, :] = ds
+                gv_ref[rows, feats] += nn(p_ref[b, part, :], ubd_ref[b])
+                gk_ref[rows, feats] += nn(ds, qbd_ref[b])
+                yield
+            gq_t = nn(kt_ref[feats, pl.ds(CHUNK * c, KEYS)], ds_ref[b])
+            fold(gq_ref, c, n, gq_t.T)
+
+        stages = (score, exponent, attend, gradient)
+        for step in range(6 + len(stages) - 1):
+            running = [
+                stage(step - i) for i, stage in enumerate(stages) if 0 <= step - i < 6
+            ]
+            while running:
+                running = [g for g in running if next(g, running) is None]
         return carry
 
     lax.fori_loop(0, 4, latitude_band, 0)
 
-    gq_low = gq_ref[...].reshape(768, D).astype(BF16)
+    gq_low = (gq_ref[...].reshape(768, D) * 0.125).astype(BF16)
     att_low = att_ref[...].reshape(768, D).astype(BF16)
 
     def put(index, value):
@@ -224,7 +237,7 @@
     put(3, tn(att_low, grad_ref[...]))
 
     def finish(i, carry):
-        rows = pl.ds(pl.multiple_of(i * 192, 192), 192)
+        rows = pl.ds(pl.multiple_of(i * 672, 672), 672)
         gk_low = gk_ref[rows, :].astype(BF16)
         gv_low = gv_ref[rows, :].astype(BF16)
         k_ref[rows, :] = gk_low
@@ -232,7 +245,7 @@
         gk_ref[rows, :] = nt(gk_low, wk_ref[...]) + nt(gv_low, wv_ref[...])
         return carry
 
-    lax.fori_loop(0, ALL // 192, finish, 0)
+    lax.fori_loop(0, ALL // 672, finish, 0)
     put(1, tn(tok_ref[...], k_ref[...]))
     put(2, tn(tok_ref[...], v_ref[...]))
     gt_own_ref[...] = gk_ref[own_rows, :] + nt(gq_low, wq_ref[...])
@@ -261,14 +274,15 @@
             pltpu.VMEM((ALL, D), F32),
             pltpu.VMEM((48, 16, D), F32),
             pltpu.VMEM((48, 16, D), F32),
-            pltpu.VMEM((3, 256, 256), BF16),
-            pltpu.VMEM((3, 256, 256), BF16),
-            pltpu.VMEM((3, 256, 256), F32),
-            pltpu.VMEM((KEYS, 512), F32),
-            pltpu.VMEM((KEYS, 256), F32),
-            pltpu.VMEM((KEYS, 256), BF16),
+            pltpu.VMEM((6, 256, 256), BF16),
+            pltpu.VMEM((6, 256, 256), BF16),
+            pltpu.VMEM((6, 256, 256), F32),
+            pltpu.VMEM((2, KEYS, 512), F32),
+            pltpu.VMEM((6, KEYS, 256), F32),
+            pltpu.VMEM((6, KEYS, 256), BF16),
+            pltpu.VMEM((6, KEYS, 256), BF16),
         ],
-        compiler_params=pltpu.CompilerParams(vmem_limit_bytes=56 * 1024 * 1024),
+        compiler_params=pltpu.CompilerParams(vmem_limit_bytes=60 * 1024 * 1024),
     )(row0, tok_wide, grad_out, w_query, w_key, w_value, w_out)
 
 

time: 173 us -> 155 us (0.90)
  Pallas kernels: 157 us -> 139 us
    pallas_call x1, Pallas kernels: 73 us -> 55.2 us  [attention(): pl.pallas_call(functools.partial(attention_kernel, lat_total), out_shape=...]
where the time goes in v3:
time: 155 us
  Pallas kernels  139 us (90%)
  local copies, waits for them, and re-layouts  13.5 us (9%)
    pallas_call x1, Pallas kernels, reduce(): pl.pallas_call(reduce_kernel, out_shape=(jax.ShapeDtypeStruct((48, 16, D)...  64.4 us
    pallas_call x1, Pallas kernels, attention(): pl.pallas_call(functools.partial(attention_kernel, lat_total), out_shape=...  55.2 us
    pallas_call x1, Pallas kernels, gather(): pl.pallas_call(gather_kernel, out_shape=jax.ShapeDtypeStruct((ALL, D), BF...  19.4 us
    unnamed x10, local copies, waits for them, and re-layouts  7.43 us

profile of v3, /device:TPU:1, one launch (start us, length us, event | category | flops | bytes accessed | tf_op | source)
XLA Modules:
  0.0 154.6 jit_solution(2122974390924405927)
XLA Ops:
  0.6 0.0 copy-start.4
  0.6 1.1 copy-done.4
  1.8 19.4 %shard_map.101.tok_ref = bf16[2688,512]{1,0:T(8,128)(2,1)S(1)} custom-call(bf16[768,512]{1,0:T(8,128)(2,1)S(1)} %bitcast.33), custom_call_target="tpu_custom_call" | custom-call | tf_op jit(solution)/shard_map/pallas_call | solution.py:402
  21.2 0.0 copy-start
  21.2 1.5 copy-done
  22.7 55.2 %shard_map.102 = (f32[768,512]{1,0:T(8,128)}, bf16[2688,512]{1,0:T(8,128)(2,1)}, bf16[4,2048,128]{2,1,0:T(8,128)(2,1)}) custom-call(s32[1]{0:T(128)} %bitcast.row0_ref, bf16[2688,512]{1,0:T(8,128)(2,1)} %copy-done, bf16[768,512]{1,0:T(8,128)(2,1)} %bitcast.39, bf16[512,512]{1,0:T(8,128)(2,1)} %wq_ref.1, bf16[512,512]{1,0:T(8,128)(2,1)} %wk_ref.1, ...), custom_call_target="tpu_custom_call" | custom-call | tf_op jit(solution)/shard_map/pallas_call | solution.py:257
  77.9 0.0 copy-start.1
  77.9 1.8 %copy-done.1 = bf16[2688,512]{1,0:T(8,128)(2,1)S(1)} copy-done((bf16[2688,512]{1,0:T(8,128)(2,1)S(1)}, bf16[2688,512]{1,0:T(8,128)(2,1)}, u32[]{:S(2)}) %copy-start.1) | copy-done | bytes 2752536
  79.7 0.0 copy-start.2
  79.7 1.6 %copy-done.2 = bf16[4,2048,128]{2,1,0:T(8,128)(2,1)S(1)} copy-done((bf16[4,2048,128]{2,1,0:T(8,128)(2,1)S(1)}, bf16[4,2048,128]{2,1,0:T(8,128)(2,1)}, u32[]{:S(2)}) %copy-start.2) | copy-done | bytes 2097176
  81.3 0.0 copy-start.3
  81.3 1.4 copy-done.3
  82.7 64.4 %shard_map.103 = (f32[48,16,512]{2,1,0:T(8,128)S(1)}, bf16[4,2048,128]{2,1,0:T(8,128)(2,1)S(1)}) custom-call(f32[48,16,512]{2,1,0:T(8,128)S(1)} %bitcast.32, bf16[2688,512]{1,0:T(8,128)(2,1)S(1)} %copy-done.1, bf16[4,2048,128]{2,1,0:T(8,128)(2,1)S(1)} %copy-done.2), custom_call_target="tpu_custom_call" | custom-call | tf_op jit(solution)/shard_map/pallas_call | solution.py:617
  147.0 1.0 convert_element_type.19
  148.1 0.4 convert_bitcast_fusion
  148.5 0.4 fusion
  148.9 0.7 copy.14
  149.5 0.7 copy.13
  150.2 1.5 copy_bitcast_fusion
  151.7 0.7 copy.12
  152.4 0.7 copy.11
  153.1 1.5 copy_bitcast_fusion.2
Async XLA Ops:
  0.6 1.1 copy-start.4
  21.2 1.5 copy-start
  77.9 1.8 %copy-start.1 = (bf16[2688,512]{1,0:T(8,128)(2,1)S(1)}, bf16[2688,512]{1,0:T(8,128)(2,1)}, u32[]{:S(2)}) copy-start(bf16[2688,512]{1,0:T(8,128)(2,1)} %get-tuple-element.11.wide_ref) | copy-start | bytes 8257540
  79.7 1.6 %copy-start.2 = (bf16[4,2048,128]{2,1,0:T(8,128)(2,1)S(1)}, bf16[4,2048,128]{2,1,0:T(8,128)(2,1)}, u32[]{:S(2)}) copy-start(bf16[4,2048,128]{2,1,0:T(8,128)(2,1)} %get-tuple-element.12.gw_ref) | copy-start | bytes 6291460
  81.3 1.4 copy-start.3

commit v4 on v2

v4 whole, which is shorter than its diff:
```python
import jax
import jax.numpy as jnp
from jax import lax
from jax.experimental import pallas as pl
from jax.experimental.pallas import tpu as pltpu
from jax.sharding import PartitionSpec as P

HEADS = 8
HEAD = 64
D = 512
RIM = 6
SPAN = 13
LATITUDES = 128
OWN = 28 * 48
SIDE = 28 * 24
ALL = OWN + 2 * SIDE
TQ = 96
KEYS = 768 + 384
CHUNK = 384
PARTS = 4
WIDTH = D // PARTS
MESH = pl.DeviceIdType.MESH
F32 = jnp.float32
BF16 = jnp.bfloat16


def nn(a, b):
    return jnp.dot(a, b, preferred_element_type=F32)


def nt(a, b):
    return lax.dot_general(a, b, (((1,), (1,)), ((), ())), preferred_element_type=F32)


def tn(a, b):
    return lax.dot_general(a, b, (((0,), (0,)), ((), ())), preferred_element_type=F32)


ORDERS = (("x", "y", "z"), ("y", "z", "x"), ("z", "x", "y"), ("x", "z", "y"))
BLOCKS = (256, 64, 16)


class Place:
    def __init__(self):
        self.lat = lax.axis_index("lat")
        self.lon = lax.axis_index("lon")
        self.z = self.lat % 4
        self.core = self.lon % 2
        self.x = self.lon // 4
        self.y = (self.lat // 4) * 2 + (self.lon // 2) % 2
        self.inside = {-1: self.lat > 0, 0: None, 1: self.lat < 7}

    def near(self, dlat, dlon):
        return (self.lat + dlat, lax.rem(self.lon + dlon + 16, 16))

    def along(self, axis, step):
        x, y, z = self.x, self.y, self.z
        if axis == "x":
            x = lax.rem(x + step, 4)
        elif axis == "y":
            y = lax.rem(y + step, 4)
        else:
            z = lax.rem(z + step, 4)
        return ((y // 2) * 4 + z, x * 4 + (y % 2) * 2 + self.core)

    def other_core(self):
        return (self.lat, self.lon + 1 - 2 * self.core)

    def index(self, axis):
        return {"x": self.x, "y": self.y, "z": self.z}[axis]


def guarded(condition, action):
    if condition is None:
        action()
    else:
        pl.when(condition)(action)


def halo_copies(place, send_sem, recv_sem, routes):
    copies = []
    for i, (dlat, dlon, source, target) in enumerate(routes):
        copy = pltpu.make_async_remote_copy(
            src_ref=source,
            dst_ref=target,
            send_sem=send_sem.at[i],
            recv_sem=recv_sem.at[i],
            device_id=place.near(dlat, dlon),
            device_id_type=MESH,
        )
        copies.append((place.inside[dlat], place.inside[-dlat], copy))
    return copies


def greet(place):
    barrier = pltpu.get_barrier_semaphore()
    for dlat in (-1, 0, 1):
        for dlon in (-1, 0, 1):
            if dlat or dlon:

                def signal(dlat=dlat, dlon=dlon):
                    pl.semaphore_signal(
                        barrier, inc=1, device_id=place.near(dlat, dlon), device_id_type=MESH
                    )

                guarded(place.inside[dlat], signal)
    rows = jnp.where(place.lat > 0, 3, 0) + jnp.where(place.lat < 7, 3, 0)
    return barrier, 2 + rows


def kernel(
    x_hbm,
    grad_hbm,
    wq_hbm,
    wk_hbm,
    wv_hbm,
    wo_hbm,
    out_ref,
    sum_ref,
    tok_ref,
    grad_ref,
    w_ref,
    k_ref,
    v_ref,
    kt_ref,
    vt_ref,
    q_ref,
    u_ref,
    gk_ref,
    gv_ref,
    gq_ref,
    att_ref,
    qbd_ref,
    ubd_ref,
    ubdt_ref,
    bias_ref,
    s_ref,
    p_ref,
    ds_ref,
    gw_ref,
    middle_ref,
    sides_ref,
    pair_ref,
    recv0,
    recv1,
    recv2,
    load_sem,
    gather_send,
    gather_recv,
    halo_send,
    halo_recv,
    pair_send,
    pair_recv,
    ring_send,
    ring_recv,
    back_send,
    back_recv,
    last_send,
    last_recv,
):
    place = Place()
    row0 = place.lat * 16
    wq_ref, wk_ref, wv_ref, wo_ref = [w_ref.at[i] for i in range(4)]
    own_rows = pl.ds(RIM * 48, 768)

    loads = [
        pltpu.make_async_copy(source, target, load_sem.at[i])
        for i, (source, target) in enumerate(
            (
                (x_hbm, tok_ref.at[own_rows]),
                (wk_hbm, wk_ref),
                (wv_hbm, wv_ref),
                (wq_hbm, wq_ref),
                (grad_hbm, grad_ref),
                (wo_hbm, wo_ref),
            )
        )
    ]
    for load in loads:
        load.start()

    barrier, count = greet(place)
    partners = [place.other_core()]
    partners += [place.along(axis, step) for axis in "xyz" for step in (1, 2, 3)]
    for partner in partners:
        pl.semaphore_signal(barrier, inc=1, device_id=partner, device_id_type=MESH)

    loads[0].wait()
    x = tok_ref[own_rows, :].astype(F32).reshape(48, 16, D)
    gw_ref[0:384, :] = x[:, 0:8].reshape(384, D).astype(BF16)
    gw_ref[384:768, :] = x[:, 8:16].reshape(384, D).astype(BF16)
    pl.semaphore_wait(barrier, count + len(partners))

    strip_first = {-1: 22, 0: 6, 1: 0}
    lat_rows = {-1: (0, 6), 0: (0, 16), 1: (10, 6)}
    routes = []
    for dlat in (-1, 0, 1):
        begin, size = lat_rows[dlat]
        for dlon in (-1, 0, 1):
            first = strip_first[dlat]
            if dlon == 0:
                if dlat == 0:
                    continue
                source = tok_ref.at[pl.ds(48 * (RIM + begin), 48 * size)]
                target = tok_ref.at[pl.ds(48 * first, 48 * size)]
            else:
                half = 384 if dlon == 1 else 0
                side = OWN if dlon == 1 else OWN + SIDE
                source = gw_ref.at[pl.ds(half + 24 * begin, 24 * size)]
                target = tok_ref.at[pl.ds(side + 24 * first, 24 * size)]
            routes.append((dlat, dlon, source, target))
    gathered = halo_copies(place, gather_send, gather_recv, routes)
    for sends, _, copy in gathered:
        guarded(sends, copy.start)

    def clear(first):
        tok_ref[pl.ds(48 * first, 288), :] = jnp.zeros((288, D), BF16)
        tok_ref[pl.ds(OWN + 24 * first, 144), :] = jnp.zeros((144, D), BF16)
        tok_ref[pl.ds(OWN + SIDE + 24 * first, 144), :] = jnp.zeros((144, D), BF16)

    pl.when(place.lat == 0)(lambda: clear(0))
    pl.when(place.lat == 7)(lambda: clear(22))

    def project(rows):
        x = tok_ref[rows, :]
        k_ref[rows, :] = nn(x, wk_ref[...]).astype(BF16)
        v_ref[rows, :] = nn(x, wv_ref[...]).astype(BF16)

    loads[1].wait()
    loads[2].wait()
    project(own_rows)
    loads[3].wait()
    q = nn(tok_ref[own_rows, :], wq_ref[...]).astype(BF16).astype(F32) * 0.125
    q_ref[...] = q.reshape(48, 16, D)
    loads[4].wait()
    loads[5].wait()
    u = nt(grad_ref[...], wo_ref[...]).astype(BF16).astype(F32)
    u_ref[...] = u.reshape(48, 16, D)

    def zero(i, carry):
        rows = pl.ds(pl.multiple_of(i * 168, 168), 168)
        gk_ref[rows, :] = jnp.zeros((168, D), F32)
        gv_ref[rows, :] = jnp.zeros((168, D), F32)
        return carry

    lax.fori_loop(0, ALL // 168, zero, 0)

    head_row = lax.broadcasted_iota(jnp.int32, (256, 256), 0)
    feature = lax.broadcasted_iota(jnp.int32, (256, 256), 1)

    def diagonal(n):
        owner = (head_row + 256 * n) // TQ
        return owner == (feature + 128 * n) // HEAD

    def band_start(r):
        lowest = jnp.where(place.lat == 0, RIM, 0)
        highest = jnp.where(place.lat == 7, RIM, 12)
        return jnp.minimum(jnp.maximum(4 * r, lowest), highest)

    def fill_bias(r):
        base = band_start(r)
        lane = lax.broadcasted_iota(jnp.int32, (1, 384), 1) % TQ
        q_lat = row0 + 4 * r + lane // 24
        first = jnp.clip(q_lat - RIM, 0, LATITUDES - SPAN) - (row0 + base - RIM)
        q_col = lane % 8

        def bias(d_lat, d_col):
            inside = (d_lat >= 0) & (d_lat < SPAN) & (d_col >= 0) & (d_col < SPAN)
            return jnp.where(inside, 0.0, -jnp.inf)

        for c in range(2):
            key = lax.broadcasted_iota(jnp.int32, (768, 1), 0)
            rows = pl.ds(CHUNK * (1 - c), 768)
            bias_ref[c, rows, :] = bias(key // 48 - first, key % 16 - 8 * c - q_col + RIM)
            key = lax.broadcasted_iota(jnp.int32, (384, 1), 0)
            rows = pl.ds(768 * c, 384)
            bias_ref[c, rows, :] = bias(key // 24 - first, key % 8 + (16 * c - 8) - q_col + RIM)

    fill_bias(0)

    for sends, receives, copy in gathered:
        guarded(sends, copy.wait_send)
        guarded(receives, copy.wait_recv)
    project(pl.ds(0, 288))
    project(pl.ds(1056, 288))
    project(pl.ds(OWN, SIDE))
    project(pl.ds(OWN + SIDE, SIDE))

    def latitude_band(r, carry):
        base = band_start(r)
        north = (place.lat == 0) & ((r == 1) | (r == 2))
        south = (place.lat == 7) & (r >= 2)
        pl.when(north | south)(lambda: fill_bias(r))
        own = [pl.multiple_of(base * 48 + 384 * i, 48) for i in range(2)]
        side = [pl.multiple_of(OWN + SIDE * c + base * 24, 48) for c in range(2)]
        for i, start in enumerate((side[0], own[0], own[1], side[1])):
            part = pl.ds(start, CHUNK)
            kt_ref[:, pl.ds(CHUNK * i, CHUNK)] = k_ref[part, :].T
            vt_ref[:, pl.ds(CHUNK * i, CHUNK)] = v_ref[part, :].T
        starts = ((side[0], own[0], own[1]), (own[0], own[1], side[1]))
        groups = pl.ds(12 * r, 12)

        for c in range(2):
            q_tile = q_ref[groups, 8 * c : 8 * c + 8, :].reshape(TQ, D).astype(BF16)
            u_tile = u_ref[groups, 8 * c : 8 * c + 8, :].reshape(TQ, D).astype(BF16)
            q_all = jnp.concatenate([q_tile] * HEADS, axis=0)
            u_all = jnp.concatenate([u_tile] * HEADS, axis=0)
            for n in range(3):
                keep = diagonal(n)
                block = q_all[256 * n : 256 * n + 256, 128 * n : 128 * n + 256]
                qbd_ref[3 * c + n] = jnp.where(keep, block, jnp.zeros_like(block))
                block = u_all[256 * n : 256 * n + 256, 128 * n : 128 * n + 256]
                block = jnp.where(keep, block, jnp.zeros_like(block))
                ubd_ref[3 * c + n] = block
                ubdt_ref[3 * c + n] = block.T
            att_ref[groups, 8 * c : 8 * c + 8, :] = jnp.zeros((12, 8, D), F32)
            gq_ref[groups, 8 * c : 8 * c + 8, :] = jnp.zeros((12, 8, D), F32)

        def fold(ref, c, n, block):
            block = jnp.where(diagonal(n), block, 0.0)
            row = 256 * n
            while row < 256 * n + 256:
                h = row // TQ
                end = min(TQ * (h + 1), 256 * n + 256)
                begin = row - TQ * h
                count = (end - row) // 8
                view = (
                    pl.ds(12 * r + begin // 8, count),
                    slice(8 * c, 8 * c + 8),
                    slice(128 * n, 128 * n + 256),
                )
                ref[view] += block[row - 256 * n : end - 256 * n].reshape(count, 8, 256)
                row = end

        state = [{} for _ in range(6)]

        def parts(b):
            return b // 3, b % 3, pl.ds(128 * (b % 3), 256)

        def score(b):
            c, n, feats = parts(b)
            bias_lanes = ((0, 128), (256, 0), (128, 256))[n]
            high = jnp.full((8, 256), -jnp.inf, F32)
            for j in range(3):
                part = pl.ds(CHUNK * j, CHUNK)
                x = nt(k_ref[pl.ds(starts[c][j], CHUNK), feats], qbd_ref[b])
                x = x + jnp.concatenate(
                    [bias_ref[c, part, pl.ds(lane, 128)] for lane in bias_lanes], axis=1
                )
                s_ref[b % 4, part, :] = x
                high = jnp.maximum(high, jnp.max(x.reshape(CHUNK // 8, 8, 256), axis=0))
                yield
            state[b]["high"] = jnp.max(high, axis=0, keepdims=True)

        def exponent(b):
            high = state[b]["high"]
            total = jnp.zeros((8, 256), F32)
            for j in range(3):
                part = pl.ds(CHUNK * j, CHUNK)
                e = jnp.exp(s_ref[b % 4, part, :] - high)
                s_ref[b % 4, part, :] = e
                total = total + jnp.sum(e.reshape(CHUNK // 8, 8, 256), axis=0)
                yield
            state[b]["scale"] = 1.0 / jnp.sum(total, axis=0, keepdims=True)

        def attend(b):
            c, n, feats = parts(b)
            scale = state[b]["scale"]
            for j in range(3):
                part = pl.ds(CHUNK * j, CHUNK)
                p = s_ref[b % 4, part, :] * scale
                s_ref[b % 4, part, :] = p
                p_ref[b % 2, part, :] = p.astype(BF16)
                yield
            out_t = nn(vt_ref[feats, pl.ds(CHUNK * c, KEYS)], p_ref[b % 2])
            out_t = out_t.astype(BF16).astype(F32)
            state[b]["row_dot"] = jnp.sum(out_t * ubdt_ref[b].astype(F32), axis=0, keepdims=True)
            fold(att_ref, c, n, out_t.T)

        def gradient(b):
            c, n, feats = parts(b)
            row_dot = state[b]["row_dot"]
            for j in range(3):
                part = pl.ds(CHUNK * j, CHUNK)
                rows = pl.ds(starts[c][j], CHUNK)
                grad_p = nt(v_ref[rows, feats], ubd_ref[b])
                ds = (s_ref[b % 4, part, :] * (grad_p - row_dot)).astype(BF16)
                ds_ref[part, :] = ds
                gv_ref[rows, feats] += nn(p_ref[b % 2, part, :], ubd_ref[b])
                gk_ref[rows, feats] += nn(ds, qbd_ref[b])
                yield
            gq_t = nn(kt_ref[feats, pl.ds(CHUNK * c, KEYS)], ds_ref[...])
            fold(gq_ref, c, n, gq_t.T)

        stages = (score, exponent, attend, gradient)
        for step in range(6 + len(stages) - 1):
            running = [
                stage(step - i) for i, stage in enumerate(stages) if 0 <= step - i < 6
            ]
            while running:
                running = [g for g in running if next(g, running) is None]
        return carry

    lax.fori_loop(0, 4, latitude_band, 0)

    def send(source, target, send_sem, recv_sem, device):
        copy = pltpu.make_async_remote_copy(
            src_ref=source,
            dst_ref=target,
            send_sem=send_sem,
            recv_sem=recv_sem,
            device_id=device,
            device_id_type=MESH,
        )
        copy.start()
        waits.append(copy)
        return copy

    waits = []

    def to_tokens(rows):
        gk_low = gk_ref[rows, :].astype(BF16)
        gv_low = gv_ref[rows, :].astype(BF16)
        return nt(gk_low, wk_ref[...]) + nt(gv_low, wv_ref[...])

    for rows in (pl.ds(OWN, SIDE), pl.ds(OWN + SIDE, SIDE), pl.ds(0, 288), pl.ds(1056, 288)):
        k_ref[rows, :] = to_tokens(rows).astype(BF16)
    strip_first = {-1: 0, 0: 6, 1: 22}
    middle_slot = {-1: 0, 1: 288}
    side_slot = {-1: 0, 0: 144, 1: 528}
    routes = []
    for dlat in (-1, 0, 1):
        size = 16 if dlat == 0 else 6
        for dlon in (-1, 0, 1):
            first = strip_first[dlat]
            if dlon == 0:
                if dlat == 0:
                    continue
                source = k_ref.at[pl.ds(48 * first, 48 * size)]
                target = middle_ref.at[pl.ds(middle_slot[dlat], 48 * size)]
            else:
                side = OWN if dlon == -1 else OWN + SIDE
                slot = SIDE if dlon == -1 else 0
                source = k_ref.at[pl.ds(side + 24 * first, 24 * size)]
                target = sides_ref.at[pl.ds(slot + side_slot[dlat], 24 * size)]
            routes.append((dlat, dlon, source, target))
    halo = halo_copies(place, halo_send, halo_recv, routes)
    for sends, _, copy in halo:
        guarded(sends, copy.start)

    gq_low = (gq_ref[...].reshape(768, D) * 0.125).astype(BF16)
    core = place.core
    pieces = (
        (core * 1536, 1536 - core * 1536, core * 512),
        (512 + core * 512, 1024 - core * 512, 512 - core * 512),
    )

    def exchange(piece):
        theirs = pl.multiple_of(pieces[piece][1], 512)
        copies = []
        for p in range(PARTS):
            columns = pl.ds(WIDTH * p, WIDTH)
            copies.append(
                send(
                    gw_ref.at[pl.ds(theirs, 512), columns],
                    pair_ref.at[piece, :, columns],
                    pair_send.at[PARTS * piece + p],
                    pair_recv.at[PARTS * piece + p],
                    place.other_core(),
                )
            )
        return copies

    gw_ref[pl.ds(0, D), :] = tn(tok_ref[own_rows, :], gq_low).astype(BF16)
    att_low = att_ref[...].reshape(768, D).astype(BF16)
    gw_ref[pl.ds(3 * D, D), :] = tn(att_low, grad_ref[...]).astype(BF16)
    first_pair = exchange(0)
    gw_ref[pl.ds(D, D), :] = tn(tok_ref[...], gk_ref[...].astype(BF16)).astype(BF16)
    gw_ref[pl.ds(2 * D, D), :] = tn(tok_ref[...], gv_ref[...].astype(BF16)).astype(BF16)
    second_pair = exchange(1)
    own = to_tokens(own_rows) + nt(gq_low, wq_ref[...])
    q_ref[...] = own.reshape(48, 16, D)

    mine = pl.multiple_of(core * 1024, 1024)
    acc_lanes = pl.ds(0, WIDTH)
    buffers = (recv0, recv1, recv2)
    staged = (0, 768, 960)
    pending = [[first_pair[p], second_pair[p]] for p in range(PARTS)]
    base = [0] * PARTS
    for stage in range(3):
        rows = BLOCKS[stage]
        incoming = buffers[stage]
        for p in range(PARTS):
            for copy in pending[p]:
                copy.wait_recv()
            if stage == 0:
                columns = pl.ds(WIDTH * p, WIDTH)
                for piece in range(2):
                    source, _, target = pieces[piece]
                    here = pl.ds(pl.multiple_of(source, 512), 512)
                    total = gw_ref[here, columns].astype(F32)
                    total = total + pair_ref[piece, :, columns].astype(F32)
                    s_ref[p, pl.ds(pl.multiple_of(target, 512), 512), acc_lanes] = total
            else:
                before = buffers[stage - 1]
                here = pl.ds(base[p], BLOCKS[stage - 1])
                total = s_ref[p, here, acc_lanes]
                for step in range(3):
                    total = total + before[p, step].astype(F32)
                s_ref[p, here, acc_lanes] = total
            axis = ORDERS[p][stage]
            me = place.index(axis)
            pending[p] = []
            for step in (1, 2, 3):
                block = base[p] + lax.rem(me + step, 4) * rows
                block = pl.multiple_of(block, rows)
                outgoing = p_ref.at[
                    p // 2,
                    pl.ds(staged[stage] + rows * (step - 1), rows),
                    pl.ds(WIDTH * (p % 2), WIDTH),
                ]
                outgoing[...] = s_ref[p, pl.ds(block, rows), acc_lanes].astype(BF16)
                slot = (p * 3 + stage) * 3 + step - 1
                pending[p].append(
                    send(
                        outgoing,
                        incoming.at[p, step - 1],
                        ring_send.at[slot],
                        ring_recv.at[slot],
                        place.along(axis, step),
                    )
                )
            base[p] = pl.multiple_of(base[p] + me * rows, rows)

    for stage in (3, 2, 1, 0):
        for p in range(PARTS):
            columns = pl.ds(WIDTH * p, WIDTH)
            for copy in pending[p]:
                copy.wait_recv()
            if stage == 3:
                total = s_ref[p, pl.ds(base[p], 16), acc_lanes]
                for step in range(3):
                    total = total + recv2[p, step].astype(F32)
                here = pl.ds(pl.multiple_of(mine + base[p], 16), 16)
                sum_ref[here, columns] = total.astype(BF16)
            if stage > 0:
                rows = BLOCKS[stage - 1]
                axis = ORDERS[p][stage - 1]
                here = pl.ds(pl.multiple_of(mine + base[p], rows), rows)
                here = sum_ref.at[here, columns]
                pending[p] = []
                for step in (1, 2, 3):
                    slot = (p * 3 + stage - 1) * 3 + step - 1
                    pending[p].append(
                        send(
                            here,
                            here,
                            back_send.at[slot],
                            back_recv.at[slot],
                            place.along(axis, step),
                        )
                    )
                base[p] = base[p] - place.index(axis) * rows
            else:
                here = sum_ref.at[pl.ds(mine, 1024), columns]
                pending[p] = [
                    send(here, here, last_send.at[p], last_recv.at[p], place.other_core())
                ]

    for sends, receives, copy in halo:
        guarded(sends, copy.wait_send)
        guarded(receives, copy.wait_recv)
    for half in range(2):
        part = sides_ref[pl.ds(SIDE * half + 144, 384), :].astype(F32).reshape(48, 8, D)
        view = q_ref[:, 8 * half : 8 * half + 8, :]
        q_ref[:, 8 * half : 8 * half + 8, :] = view + part

    def edge(slot, side, first):
        rows = pl.ds(3 * first, 18)
        part = middle_ref[pl.ds(slot, 288), :].astype(F32).reshape(18, 16, D)
        q_ref[rows] = q_ref[rows] + part
        for half in range(2):
            part = sides_ref[pl.ds(SIDE * half + side, 144), :].astype(F32).reshape(18, 8, D)
            view = q_ref[rows, 8 * half : 8 * half + 8, :]
            q_ref[rows, 8 * half : 8 * half + 8, :] = view + part

    pl.when(place.lat < 7)(lambda: edge(0, 0, 10))
    pl.when(place.lat > 0)(lambda: edge(288, 528, 0))
    out_ref[...] = q_ref[...].reshape(768, D).astype(BF16)

    for p in range(PARTS):
        pending[p][0].wait_recv()
    for copy in waits:
        copy.wait_send()


def whole(x, g, w_query, w_key, w_value, w_out):
    dma = pltpu.SemaphoreType.DMA
    shapes = [
        ((ALL, D), BF16),
        ((768, D), BF16),
        ((4, D, D), BF16),
        ((ALL, D), BF16),
        ((ALL, D), BF16),
        ((D, 1536), BF16),
        ((D, 1536), BF16),
        ((48, 16, D), F32),
        ((48, 16, D), F32),
        ((ALL, D), F32),
        ((ALL, D), F32),
        ((48, 16, D), F32),
        ((48, 16, D), F32),
        ((6, 256, 256), BF16),
        ((6, 256, 256), BF16),
        ((6, 256, 256), BF16),
        ((2, KEYS, 384), F32),
        ((4, KEYS, 256), F32),
        ((2, KEYS, 256), BF16),
        ((KEYS, 256), BF16),
        ((4 * D, D), BF16),
        ((576, D), BF16),
        ((2 * SIDE, D), BF16),
        ((2, D, D), BF16),
    ]
    for rows in BLOCKS:
        shapes.append(((PARTS, 3, rows, WIDTH), BF16))
    scratch = [pltpu.VMEM(shape, kind) for shape, kind in shapes]
    scratch.append(dma((6,)))
    for count in (8, 8, 2 * PARTS, 9 * PARTS, 9 * PARTS, PARTS):
        scratch += [dma((count,))] * 2
    return pl.pallas_call(
        kernel,
        out_shape=(
            jax.ShapeDtypeStruct((768, D), BF16),
            jax.ShapeDtypeStruct((4 * D, D), BF16),
        ),
        in_specs=[pl.BlockSpec(memory_space=pl.ANY)] * 6,
        out_specs=(pl.BlockSpec(memory_space=pltpu.VMEM),) * 2,
        scratch_shapes=scratch,
        compiler_params=pltpu.CompilerParams(
            collective_id=0, has_side_effects=True, vmem_limit_bytes=62 * 1024 * 1024
        ),
    )(x, g, w_query, w_key, w_value, w_out)


def on_device(tokens, w_query, w_key, w_value, w_out, grad_out):
    x = tokens.transpose(0, 2, 1, 3).reshape(768, D)
    g = grad_out.transpose(0, 2, 1, 3).reshape(768, D)
    grad_tokens, sums = whole(x, g, w_query, w_key, w_value, w_out)
    grad_tokens = grad_tokens.reshape(16, 3, 16, D).transpose(0, 2, 1, 3)
    sums = sums.reshape(4, D, D).astype(F32)
    return grad_tokens, sums[0], sums[1], sums[2], sums[3]


def solution(mesh):
    placed = (P("lat", "lon", None, None), P(), P(), P(), P(), P("lat", "lon", None, None))
    return jax.shard_map(
        on_device,
        mesh=mesh,
        in_specs=placed,
        out_specs=(P("lat", "lon", None, None), P(), P(), P(), P()),
        check_vma=False,
    )
```

time: 173 us -> 131 us (0.76)
  Pallas kernels: 157 us -> 125 us
  local copies, waits for them, and re-layouts: 13.5 us -> 4.71 us
    pallas_call x3 -> x1, Pallas kernels: 157 us -> 125 us  [whole(): pl.pallas_call(kernel, out_shape=(jax.ShapeDtypeStruct((768, D), BF16), j...]
    unnamed x10 -> x3, local copies, waits for them, and re-layouts: 7.43 us -> 0.88 us
    squeeze x2 -> x0, local copies, waits for them, and re-layouts: 2.97 us -> none  [on_device(): return (grad_tokens, sums[0], sums[1], sums[2], sums[3])]
    slice x5 -> x1, local copies, waits for them, and re-layouts: 3.09 us -> 3.82 us  [on_device(): return (grad_tokens, sums[0], sums[1], sums[2], sums[3])]
where the time goes in v4:
time: 131 us
  Pallas kernels  125 us (95%)
  local copies, waits for them, and re-layouts  4.71 us (4%)
    pallas_call x1, Pallas kernels, whole(): pl.pallas_call(kernel, out_shape=(jax.ShapeDtypeStruct((768, D), BF16), j...  125 us
    slice x1, local copies, waits for them, and re-layouts, on_device(): return (grad_tokens, sums[0], sums[1], sums[2], sums[3])  3.82 us

profile of v4, /device:TPU:1, one launch (start us, length us, event | category | flops | bytes accessed | tf_op | source)
XLA Modules:
  0.0 130.5 jit_solution(11290825059455524654)
XLA Ops:
  0.6 125.2 %shard_map.101 = (bf16[768,512]{1,0:T(8,128)(2,1)}, bf16[2048,512]{1,0:T(8,128)(2,1)}) custom-call(bf16[768,512]{1,0:T(8,128)(2,1)} %bitcast.9, bf16[768,512]{1,0:T(8,128)(2,1)} %bitcast.10, bf16[512,512]{1,0:T(8,128)(2,1)} %wq_hbm.1, bf16[512,512]{1,0:T(8,128)(2,1)} %wk_hbm.1, bf16[512,512]{1,0:T(8,128)(2,1)} %wv_hbm.1, bf16[512,512]{1,0:T(8,128)(2,1)} %wo_hbm.1), custom_call_target="tpu_custom_call" | custom-call | tf_op jit(solution)/shard_map/pallas_call | solution.py:631
  125.8 0.0 copy-start
  125.8 3.8 %fusion = (f32[512,512]{1,0:T(8,128)}, f32[512,512]{1,0:T(8,128)}, f32[512,512]{1,0:T(8,128)}, f32[512,512]{1,0:T(8,128)}) fusion(bf16[2048,512]{1,0:T(8,128)(2,1)} %get-tuple-element.8), kind=kLoop, calls=%fused_computation | loop fusion | bytes 8388608 | tf_op jit(solution)/shard_map/slice | solution.py:652
  129.7 0.0 copy-done
  129.7 0.9 copy.12
Async XLA Ops:
  125.8 3.8 %copy-start = (bf16[768,512]{1,0:T(8,128)(2,1)S(1)}, bf16[768,512]{1,0:T(8,128)(2,1)}, u32[]{:S(2)}) copy-start(bf16[768,512]{1,0:T(8,128)(2,1)} %get-tuple-element.7) | copy-start | bytes 2359300

commit v5 on v4

--- a/solution.py
+++ b/solution.py
@@ -36,7 +36,7 @@
     return lax.dot_general(a, b, (((0,), (0,)), ((), ())), preferred_element_type=F32)
 
 
-ORDERS = (("x", "y", "z"), ("y", "z", "x"), ("z", "x", "y"), ("x", "z", "y"))
+ORDERS = (("x", "z", "y"), ("z", "x", "y"), ("x", "y", "z"), ("z", "y", "x"))
 BLOCKS = (256, 64, 16)
 
 
@@ -88,7 +88,7 @@
             device_id=place.near(dlat, dlon),
             device_id_type=MESH,
         )
-        copies.append((place.inside[dlat], place.inside[-dlat], copy))
+        copies.append((dlat, place.inside[dlat], copy))
     return copies
 
 
@@ -210,7 +210,7 @@
                 target = tok_ref.at[pl.ds(side + 24 * first, 24 * size)]
             routes.append((dlat, dlon, source, target))
     gathered = halo_copies(place, gather_send, gather_recv, routes)
-    for sends, _, copy in gathered:
+    for dlat, sends, copy in gathered:
         guarded(sends, copy.start)
 
     def clear(first):
@@ -276,21 +276,36 @@
             rows = pl.ds(768 * c, 384)
             bias_ref[c, rows, :] = bias(key // 24 - first, key % 8 + (16 * c - 8) - q_col + RIM)
 
-    fill_bias(0)
-
-    for sends, receives, copy in gathered:
-        guarded(sends, copy.wait_send)
-        guarded(receives, copy.wait_recv)
-    project(pl.ds(0, 288))
-    project(pl.ds(1056, 288))
-    project(pl.ds(OWN, SIDE))
-    project(pl.ds(OWN + SIDE, SIDE))
-
-    def latitude_band(r, carry):
+    fill_bias(jnp.where(place.lat < 4, 0, 3))
+
+    upward = place.lat < 4
+    for dlat, _, copy in gathered:
+        if dlat == 0:
+            copy.wait_recv()
+        elif dlat == 1:
+            pl.when(upward & (place.lat > 0))(copy.wait_recv)
+        else:
+            pl.when((place.lat >= 4) & (place.lat < 7))(copy.wait_recv)
+    project(pl.ds(pl.multiple_of(jnp.where(upward, 0, 1056), 96), 288))
+    for side in (OWN, OWN + SIDE):
+        project(pl.ds(pl.multiple_of(side + jnp.where(upward, 0, 144), 48), 528))
+
+    def late_halo():
+        for dlat, _, copy in gathered:
+            if dlat == 1:
+                pl.when(place.lat >= 4)(copy.wait_recv)
+            elif dlat == -1:
+                pl.when(upward)(copy.wait_recv)
+        project(pl.ds(pl.multiple_of(jnp.where(upward, 1056, 0), 96), 288))
+        for side in (OWN, OWN + SIDE):
+            project(pl.ds(pl.multiple_of(side + jnp.where(upward, 528, 0), 48), 144))
+
+    def latitude_band(i, carry):
+        r = jnp.where(upward, i, 3 - i)
         base = band_start(r)
-        north = (place.lat == 0) & ((r == 1) | (r == 2))
-        south = (place.lat == 7) & (r >= 2)
-        pl.when(north | south)(lambda: fill_bias(r))
+        pole = (place.lat == 0) | (place.lat == 7)
+        pl.when(pole & ((i == 1) | (i == 2)))(lambda: fill_bias(r))
+        pl.when(i == 2)(late_halo)
         own = [pl.multiple_of(base * 48 + 384 * i, 48) for i in range(2)]
         side = [pl.multiple_of(OWN + SIDE * c + base * 24, 48) for c in range(2)]
         for i, start in enumerate((side[0], own[0], own[1], side[1])):
@@ -423,30 +438,20 @@
         gv_low = gv_ref[rows, :].astype(BF16)
         return nt(gk_low, wk_ref[...]) + nt(gv_low, wv_ref[...])
 
-    for rows in (pl.ds(OWN, SIDE), pl.ds(OWN + SIDE, SIDE), pl.ds(0, 288), pl.ds(1056, 288)):
-        k_ref[rows, :] = to_tokens(rows).astype(BF16)
-    strip_first = {-1: 0, 0: 6, 1: 22}
-    middle_slot = {-1: 0, 1: 288}
-    side_slot = {-1: 0, 0: 144, 1: 528}
-    routes = []
-    for dlat in (-1, 0, 1):
-        size = 16 if dlat == 0 else 6
-        for dlon in (-1, 0, 1):
-            first = strip_first[dlat]
-            if dlon == 0:
-                if dlat == 0:
-                    continue
-                source = k_ref.at[pl.ds(48 * first, 48 * size)]
-                target = middle_ref.at[pl.ds(middle_slot[dlat], 48 * size)]
-            else:
-                side = OWN if dlon == -1 else OWN + SIDE
-                slot = SIDE if dlon == -1 else 0
-                source = k_ref.at[pl.ds(side + 24 * first, 24 * size)]
-                target = sides_ref.at[pl.ds(slot + side_slot[dlat], 24 * size)]
-            routes.append((dlat, dlon, source, target))
-    halo = halo_copies(place, halo_send, halo_recv, routes)
-    for sends, _, copy in halo:
-        guarded(sends, copy.start)
+    for dlat, sends, copy in gathered:
+        guarded(sends, copy.wait_send)
+    along_lon = []
+    for i, (dlon, source, target) in enumerate(((-1, OWN, SIDE), (1, OWN + SIDE, 0))):
+        k_ref[pl.ds(source, SIDE), :] = to_tokens(pl.ds(source, SIDE)).astype(BF16)
+        along_lon.append(
+            send(
+                k_ref.at[pl.ds(source, SIDE)],
+                sides_ref.at[pl.ds(target, SIDE)],
+                halo_send.at[i],
+                halo_recv.at[i],
+                place.near(0, dlon),
+            )
+        )
 
     gq_low = (gq_ref[...].reshape(768, D) * 0.125).astype(BF16)
     core = place.core
@@ -478,8 +483,37 @@
     gw_ref[pl.ds(D, D), :] = tn(tok_ref[...], gk_ref[...].astype(BF16)).astype(BF16)
     gw_ref[pl.ds(2 * D, D), :] = tn(tok_ref[...], gv_ref[...].astype(BF16)).astype(BF16)
     second_pair = exchange(1)
+    u_ref[0:18] = to_tokens(pl.ds(0, 288)).reshape(18, 16, D)
+    u_ref[18:36] = to_tokens(pl.ds(1056, 288)).reshape(18, 16, D)
     own = to_tokens(own_rows) + nt(gq_low, wq_ref[...])
     q_ref[...] = own.reshape(48, 16, D)
+
+    for copy in along_lon:
+        copy.wait_recv()
+
+    def add_sides(ref, group, row, groups):
+        for half in range(2):
+            part = sides_ref[pl.ds(SIDE * half + row, 8 * groups), :].astype(F32)
+            view = (pl.ds(group, groups), slice(8 * half, 8 * half + 8), slice(None))
+            ref[view] = ref[view] + part.reshape(groups, 8, D)
+
+    add_sides(u_ref, 0, 0, 18)
+    add_sides(u_ref, 18, 528, 18)
+    along_lat = []
+    for i, dlat in enumerate((-1, 1)):
+        strip = u_ref[pl.ds(18 * i, 18)].reshape(288, D).astype(BF16)
+        k_ref[pl.ds(288 * i, 288), :] = strip
+        copy = pltpu.make_async_remote_copy(
+            src_ref=k_ref.at[pl.ds(288 * i, 288)],
+            dst_ref=middle_ref.at[pl.ds(288 * i, 288)],
+            send_sem=halo_send.at[2 + i],
+            recv_sem=halo_recv.at[2 + i],
+            device_id=place.near(dlat, 0),
+            device_id_type=MESH,
+        )
+        guarded(place.inside[dlat], copy.start)
+        along_lat.append((place.inside[dlat], place.inside[-dlat], copy))
+    add_sides(q_ref, 0, 144, 48)
 
     mine = pl.multiple_of(core * 1024, 1024)
     acc_lanes = pl.ds(0, WIDTH)
@@ -567,25 +601,17 @@
                     send(here, here, last_send.at[p], last_recv.at[p], place.other_core())
                 ]
 
-    for sends, receives, copy in halo:
+    for sends, receives, copy in along_lat:
         guarded(sends, copy.wait_send)
         guarded(receives, copy.wait_recv)
-    for half in range(2):
-        part = sides_ref[pl.ds(SIDE * half + 144, 384), :].astype(F32).reshape(48, 8, D)
-        view = q_ref[:, 8 * half : 8 * half + 8, :]
-        q_ref[:, 8 * half : 8 * half + 8, :] = view + part
-
-    def edge(slot, side, first):
+
+    def edge(slot, first):
         rows = pl.ds(3 * first, 18)
         part = middle_ref[pl.ds(slot, 288), :].astype(F32).reshape(18, 16, D)
         q_ref[rows] = q_ref[rows] + part
-        for half in range(2):
-            part = sides_ref[pl.ds(SIDE * half + side, 144), :].astype(F32).reshape(18, 8, D)
-            view = q_ref[rows, 8 * half : 8 * half + 8, :]
-            q_ref[rows, 8 * half : 8 * half + 8, :] = view + part
-
-    pl.when(place.lat < 7)(lambda: edge(0, 0, 10))
-    pl.when(place.lat > 0)(lambda: edge(288, 528, 0))
+
+    pl.when(place.lat < 7)(lambda: edge(0, 10))
+    pl.when(place.lat > 0)(lambda: edge(288, 0))
     out_ref[...] = q_ref[...].reshape(768, D).astype(BF16)
 
     for p in range(PARTS):
@@ -626,7 +652,7 @@
         shapes.append(((PARTS, 3, rows, WIDTH), BF16))
     scratch = [pltpu.VMEM(shape, kind) for shape, kind in shapes]
     scratch.append(dma((6,)))
-    for count in (8, 8, 2 * PARTS, 9 * PARTS, 9 * PARTS, PARTS):
+    for count in (8, 4, 2 * PARTS, 9 * PARTS, 9 * PARTS, PARTS):
         scratch += [dma((count,))] * 2
     return pl.pallas_call(
         kernel,

time: 131 us -> 123 us (0.939)
  Pallas kernels: 125 us -> 118 us
    pallas_call x1, Pallas kernels: 125 us -> 118 us  [whole(): pl.pallas_call(kernel, out_shape=(jax.ShapeDtypeStruct((768, D), BF16), j...]
where the time goes in v5:
time: 123 us
  Pallas kernels  118 us (96%)
  local copies, waits for them, and re-layouts  4.71 us (4%)
    pallas_call x1, Pallas kernels, whole(): pl.pallas_call(kernel, out_shape=(jax.ShapeDtypeStruct((768, D), BF16), j...  118 us
    slice x1, local copies, waits for them, and re-layouts, on_device(): return (grad_tokens, sums[0], sums[1], sums[2], sums[3])  3.82 us

profile of v5, /device:TPU:1, one launch (start us, length us, event | category | flops | bytes accessed | tf_op | source)
XLA Modules:
  0.0 123.2 jit_solution(15205834662904635955)
XLA Ops:
  0.6 117.9 %shard_map.101 = (bf16[768,512]{1,0:T(8,128)(2,1)}, bf16[2048,512]{1,0:T(8,128)(2,1)}) custom-call(bf16[768,512]{1,0:T(8,128)(2,1)} %bitcast.9, bf16[768,512]{1,0:T(8,128)(2,1)} %bitcast.10, bf16[512,512]{1,0:T(8,128)(2,1)} %wq_hbm.1, bf16[512,512]{1,0:T(8,128)(2,1)} %wk_hbm.1, bf16[512,512]{1,0:T(8,128)(2,1)} %wv_hbm.1, bf16[512,512]{1,0:T(8,128)(2,1)} %wo_hbm.1), custom_call_target="tpu_custom_call" | custom-call | tf_op jit(solution)/shard_map/pallas_call | solution.py:657
  118.5 0.0 copy-start
  118.5 3.8 %fusion = (f32[512,512]{1,0:T(8,128)}, f32[512,512]{1,0:T(8,128)}, f32[512,512]{1,0:T(8,128)}, f32[512,512]{1,0:T(8,128)}) fusion(bf16[2048,512]{1,0:T(8,128)(2,1)} %get-tuple-element.8), kind=kLoop, calls=%fused_computation | loop fusion | bytes 8388608 | tf_op jit(solution)/shard_map/slice | solution.py:678
  122.4 0.0 copy-done
  122.4 0.9 copy.12
Async XLA Ops:
  118.5 3.8 %copy-start = (bf16[768,512]{1,0:T(8,128)(2,1)S(1)}, bf16[768,512]{1,0:T(8,128)(2,1)}, u32[]{:S(2)}) copy-start(bf16[768,512]{1,0:T(8,128)(2,1)} %get-tuple-element.7) | copy-start | bytes 2359300

commit v6 on v5

--- a/solution.py
+++ b/solution.py
@@ -17,8 +17,7 @@
 TQ = 96
 KEYS = 768 + 384
 CHUNK = 384
-PARTS = 4
-WIDTH = D // PARTS
+PARTS = 2
 MESH = pl.DeviceIdType.MESH
 F32 = jnp.float32
 BF16 = jnp.bfloat16
@@ -36,8 +35,8 @@
     return lax.dot_general(a, b, (((0,), (0,)), ((), ())), preferred_element_type=F32)
 
 
-ORDERS = (("x", "z", "y"), ("z", "x", "y"), ("x", "y", "z"), ("z", "y", "x"))
-BLOCKS = (256, 64, 16)
+AXES = (("x", "yz"), ("z", "yx"))
+STEPS = [(i, j) for i in range(4) for j in range(4) if i or j]
 
 
 class Place:
@@ -53,14 +52,10 @@
     def near(self, dlat, dlon):
         return (self.lat + dlat, lax.rem(self.lon + dlon + 16, 16))
 
-    def along(self, axis, step):
-        x, y, z = self.x, self.y, self.z
-        if axis == "x":
-            x = lax.rem(x + step, 4)
-        elif axis == "y":
-            y = lax.rem(y + step, 4)
-        else:
-            z = lax.rem(z + step, 4)
+    def along(self, **steps):
+        x = lax.rem(self.x + steps.get("x", 0), 4)
+        y = lax.rem(self.y + steps.get("y", 0), 4)
+        z = lax.rem(self.z + steps.get("z", 0), 4)
         return ((y // 2) * 4 + z, x * 4 + (y % 2) * 2 + self.core)
 
     def other_core(self):
@@ -143,7 +138,6 @@
     pair_ref,
     recv0,
     recv1,
-    recv2,
     load_sem,
     gather_send,
     gather_recv,
@@ -153,8 +147,12 @@
     pair_recv,
     ring_send,
     ring_recv,
+    plane_send,
+    plane_recv,
     back_send,
     back_recv,
+    ring_back_send,
+    ring_back_recv,
     last_send,
     last_recv,
 ):
@@ -181,7 +179,8 @@
 
     barrier, count = greet(place)
     partners = [place.other_core()]
-    partners += [place.along(axis, step) for axis in "xyz" for step in (1, 2, 3)]
+    partners += [place.along(y=i, z=j) for i, j in STEPS]
+    partners += [place.along(y=i, x=j) for i, j in STEPS if j]
     for partner in partners:
         pl.semaphore_signal(barrier, inc=1, device_id=partner, device_id_type=MESH)
 
@@ -456,37 +455,139 @@
     gq_low = (gq_ref[...].reshape(768, D) * 0.125).astype(BF16)
     core = place.core
     pieces = (
-        (core * 1536, 1536 - core * 1536, core * 512),
-        (512 + core * 512, 1024 - core * 512, 512 - core * 512),
+        (core * 1536, 1536 - core * 1536),
+        (512 + core * 512, 1024 - core * 512),
     )
 
-    def exchange(piece):
-        theirs = pl.multiple_of(pieces[piece][1], 512)
-        copies = []
-        for p in range(PARTS):
-            columns = pl.ds(WIDTH * p, WIDTH)
-            copies.append(
+    first_rows = [pl.multiple_of(piece[0], 512) for piece in pieces]
+    pending = [None] * PARTS
+    quarter = [pl.multiple_of(place.index(AXES[p][0]) * 128, 128) for p in range(PARTS)]
+    slot_rows = []
+    slot_lanes = []
+    for p in range(PARTS):
+        one, two = AXES[p][1]
+        index = place.index(one) * 4 + place.index(two)
+        slot_rows.append(pl.multiple_of(index // 2 * 16, 16))
+        slot_lanes.append(pl.multiple_of(index % 2 * 256, 256))
+    totals = (gq_ref, att_ref)
+
+    def exchange(p):
+        theirs = pl.multiple_of(pieces[p][1], 512)
+        source = gw_ref.at[pl.ds(theirs, 512)]
+        pending[p] = [
+            send(source, pair_ref.at[p], pair_send.at[p], pair_recv.at[p], place.other_core())
+        ]
+
+    def arrive(p):
+        for copy in pending[p]:
+            copy.wait_recv()
+        pending[p] = []
+
+    def ring(p):
+        arrive(p)
+        total = gw_ref[pl.ds(first_rows[p], 512), :].astype(F32) + pair_ref[p].astype(F32)
+        totals[p][0:32] = total.reshape(32, 16, D)
+        axis = AXES[p][0]
+        me = place.index(axis)
+        for step in (1, 2, 3):
+            block = lax.rem(me + step, 4) * 8
+            outgoing = v_ref.at[pl.ds(1024 * p + 128 * (step - 1), 128)]
+            outgoing[...] = totals[p][pl.ds(block, 8)].reshape(128, D).astype(BF16)
+            slot = p * 3 + step - 1
+            pending[p].append(
                 send(
-                    gw_ref.at[pl.ds(theirs, 512), columns],
-                    pair_ref.at[piece, :, columns],
-                    pair_send.at[PARTS * piece + p],
-                    pair_recv.at[PARTS * piece + p],
-                    place.other_core(),
+                    outgoing,
+                    recv0.at[p, step - 1],
+                    ring_send.at[slot],
+                    ring_recv.at[slot],
+                    place.along(**{axis: step}),
                 )
             )
-        return copies
+
+    def plane(p):
+        arrive(p)
+        axis = AXES[p][0]
+        here = pl.ds(place.index(axis) * 8, 8)
+        total = totals[p][here].reshape(128, D)
+        for step in range(3):
+            total = total + recv0[p, step].astype(F32)
+        totals[p][here] = total.reshape(8, 16, D)
+        first = 1024 * p + 384
+        v_ref[pl.ds(first, 128), :] = total.astype(BF16)
+        one, two = AXES[p][1]
+        a, b = place.index(one), place.index(two)
+        for k, (i, j) in enumerate(STEPS):
+            block = lax.rem(a + i, 4) * 4 + lax.rem(b + j, 4)
+            row = pl.multiple_of(first + block // 2 * 16, 16)
+            lane = pl.multiple_of(block % 2 * 256, 256)
+            slot = p * 15 + k
+            pending[p].append(
+                send(
+                    v_ref.at[pl.ds(row, 16), pl.ds(lane, 256)],
+                    recv1.at[p, k],
+                    plane_send.at[slot],
+                    plane_recv.at[slot],
+                    place.along(**{one: i, two: j}),
+                )
+            )
+
+    def plane_back(p):
+        arrive(p)
+        lanes = pl.ds(slot_lanes[p], 256)
+        group = place.index(AXES[p][0]) * 8 + slot_rows[p] // 16
+        total = totals[p][group, :, lanes]
+        for k in range(15):
+            total = total + recv1[p, k].astype(F32)
+        row = pl.multiple_of(first_rows[p] + quarter[p] + slot_rows[p], 16)
+        sum_ref[pl.ds(row, 16), lanes] = total.astype(BF16)
+        here = sum_ref.at[pl.ds(row, 16), lanes]
+        one, two = AXES[p][1]
+        for k, (i, j) in enumerate(STEPS):
+            slot = p * 15 + k
+            pending[p].append(
+                send(
+                    here,
+                    here,
+                    back_send.at[slot],
+                    back_recv.at[slot],
+                    place.along(**{one: i, two: j}),
+                )
+            )
+
+    def ring_back(p):
+        arrive(p)
+        here = sum_ref.at[pl.ds(pl.multiple_of(first_rows[p] + quarter[p], 128), 128)]
+        for step in (1, 2, 3):
+            slot = p * 3 + step - 1
+            pending[p].append(
+                send(
+                    here,
+                    here,
+                    ring_back_send.at[slot],
+                    ring_back_recv.at[slot],
+                    place.along(**{AXES[p][0]: step}),
+                )
+            )
+
+    def pair_back(p):
+        arrive(p)
+        here = sum_ref.at[pl.ds(first_rows[p], 512)]
+        pending[p] = [send(here, here, last_send.at[p], last_recv.at[p], place.other_core())]
 
     gw_ref[pl.ds(0, D), :] = tn(tok_ref[own_rows, :], gq_low).astype(BF16)
     att_low = att_ref[...].reshape(768, D).astype(BF16)
     gw_ref[pl.ds(3 * D, D), :] = tn(att_low, grad_ref[...]).astype(BF16)
-    first_pair = exchange(0)
+    exchange(0)
     gw_ref[pl.ds(D, D), :] = tn(tok_ref[...], gk_ref[...].astype(BF16)).astype(BF16)
     gw_ref[pl.ds(2 * D, D), :] = tn(tok_ref[...], gv_ref[...].astype(BF16)).astype(BF16)
-    second_pair = exchange(1)
+    exchange(1)
+    ring(0)
     u_ref[0:18] = to_tokens(pl.ds(0, 288)).reshape(18, 16, D)
     u_ref[18:36] = to_tokens(pl.ds(1056, 288)).reshape(18, 16, D)
     own = to_tokens(own_rows) + nt(gq_low, wq_ref[...])
     q_ref[...] = own.reshape(48, 16, D)
+    ring(1)
+    plane(0)
 
     for copy in along_lon:
         copy.wait_recv()
@@ -515,91 +616,13 @@
         along_lat.append((place.inside[dlat], place.inside[-dlat], copy))
     add_sides(q_ref, 0, 144, 48)
 
-    mine = pl.multiple_of(core * 1024, 1024)
-    acc_lanes = pl.ds(0, WIDTH)
-    buffers = (recv0, recv1, recv2)
-    staged = (0, 768, 960)
-    pending = [[first_pair[p], second_pair[p]] for p in range(PARTS)]
-    base = [0] * PARTS
-    for stage in range(3):
-        rows = BLOCKS[stage]
-        incoming = buffers[stage]
-        for p in range(PARTS):
-            for copy in pending[p]:
-                copy.wait_recv()
-            if stage == 0:
-                columns = pl.ds(WIDTH * p, WIDTH)
-                for piece in range(2):
-                    source, _, target = pieces[piece]
-                    here = pl.ds(pl.multiple_of(source, 512), 512)
-                    total = gw_ref[here, columns].astype(F32)
-                    total = total + pair_ref[piece, :, columns].astype(F32)
-                    s_ref[p, pl.ds(pl.multiple_of(target, 512), 512), acc_lanes] = total
-            else:
-                before = buffers[stage - 1]
-                here = pl.ds(base[p], BLOCKS[stage - 1])
-                total = s_ref[p, here, acc_lanes]
-                for step in range(3):
-                    total = total + before[p, step].astype(F32)
-                s_ref[p, here, acc_lanes] = total
-            axis = ORDERS[p][stage]
-            me = place.index(axis)
-            pending[p] = []
-            for step in (1, 2, 3):
-                block = base[p] + lax.rem(me + step, 4) * rows
-                block = pl.multiple_of(block, rows)
-                outgoing = p_ref.at[
-                    p // 2,
-                    pl.ds(staged[stage] + rows * (step - 1), rows),
-                    pl.ds(WIDTH * (p % 2), WIDTH),
-                ]
-                outgoing[...] = s_ref[p, pl.ds(block, rows), acc_lanes].astype(BF16)
-                slot = (p * 3 + stage) * 3 + step - 1
-                pending[p].append(
-                    send(
-                        outgoing,
-                        incoming.at[p, step - 1],
-                        ring_send.at[slot],
-                        ring_recv.at[slot],
-                        place.along(axis, step),
-                    )
-                )
-            base[p] = pl.multiple_of(base[p] + me * rows, rows)
-
-    for stage in (3, 2, 1, 0):
-        for p in range(PARTS):
-            columns = pl.ds(WIDTH * p, WIDTH)
-            for copy in pending[p]:
-                copy.wait_recv()
-            if stage == 3:
-                total = s_ref[p, pl.ds(base[p], 16), acc_lanes]
-                for step in range(3):
-                    total = total + recv2[p, step].astype(F32)
-                here = pl.ds(pl.multiple_of(mine + base[p], 16), 16)
-                sum_ref[here, columns] = total.astype(BF16)
-            if stage > 0:
-                rows = BLOCKS[stage - 1]
-                axis = ORDERS[p][stage - 1]
-                here = pl.ds(pl.multiple_of(mine + base[p], rows), rows)
-                here = sum_ref.at[here, columns]
-                pending[p] = []
-                for step in (1, 2, 3):
-                    slot = (p * 3 + stage - 1) * 3 + step - 1
-                    pending[p].append(
-                        send(
-                            here,
-                            here,
-                            back_send.at[slot],
-                            back_recv.at[slot],
-                            place.along(axis, step),
-                        )
-                    )
-                base[p] = base[p] - place.index(axis) * rows
-            else:
-                here = sum_ref.at[pl.ds(mine, 1024), columns]
-                pending[p] = [
-                    send(here, here, last_send.at[p], last_recv.at[p], place.other_core())
-                ]
+    plane_back(0)
+    plane(1)
+    ring_back(0)
+    plane_back(1)
+    pair_back(0)
+    ring_back(1)
+    pair_back(1)
 
     for sends, receives, copy in along_lat:
         guarded(sends, copy.wait_send)
@@ -648,11 +671,10 @@
         ((2 * SIDE, D), BF16),
         ((2, D, D), BF16),
     ]
-    for rows in BLOCKS:
-        shapes.append(((PARTS, 3, rows, WIDTH), BF16))
+    shapes += [((PARTS, 3, 128, D), BF16), ((PARTS, 15, 16, 256), BF16)]
     scratch = [pltpu.VMEM(shape, kind) for shape, kind in shapes]
     scratch.append(dma((6,)))
-    for count in (8, 4, 2 * PARTS, 9 * PARTS, 9 * PARTS, PARTS):
+    for count in (8, 4, PARTS, 3 * PARTS, 15 * PARTS, 15 * PARTS, 3 * PARTS, PARTS):
         scratch += [dma((count,))] * 2
     return pl.pallas_call(
         kernel,

time: 123 us -> 120 us (0.976)
  Pallas kernels: 118 us -> 114 us
    pallas_call x1, Pallas kernels: 118 us -> 114 us  [whole(): pl.pallas_call(kernel, out_shape=(jax.ShapeDtypeStruct((768, D), BF16), j...]
where the time goes in v6:
time: 120 us
  Pallas kernels  114 us (95%)
  local copies, waits for them, and re-layouts  4.71 us (4%)
    pallas_call x1, Pallas kernels, whole(): pl.pallas_call(kernel, out_shape=(jax.ShapeDtypeStruct((768, D), BF16), j...  114 us
    slice x1, local copies, waits for them, and re-layouts, on_device(): return (grad_tokens, sums[0], sums[1], sums[2], sums[3])  3.82 us

profile of v6, /device:TPU:1, one launch (start us, length us, event | category | flops | bytes accessed | tf_op | source)
XLA Modules:
  0.0 119.7 jit_solution(1283898121142282793)
XLA Ops:
  0.6 114.3 %shard_map.101 = (bf16[768,512]{1,0:T(8,128)(2,1)}, bf16[2048,512]{1,0:T(8,128)(2,1)}) custom-call(bf16[768,512]{1,0:T(8,128)(2,1)} %bitcast.9, bf16[768,512]{1,0:T(8,128)(2,1)} %bitcast.10, bf16[512,512]{1,0:T(8,128)(2,1)} %wq_hbm.1, bf16[512,512]{1,0:T(8,128)(2,1)} %wk_hbm.1, bf16[512,512]{1,0:T(8,128)(2,1)} %wv_hbm.1, bf16[512,512]{1,0:T(8,128)(2,1)} %wo_hbm.1), custom_call_target="tpu_custom_call" | custom-call | tf_op jit(solution)/shard_map/pallas_call | solution.py:679
  115.0 0.0 copy-start
  115.0 3.8 %fusion = (f32[512,512]{1,0:T(8,128)}, f32[512,512]{1,0:T(8,128)}, f32[512,512]{1,0:T(8,128)}, f32[512,512]{1,0:T(8,128)}) fusion(bf16[2048,512]{1,0:T(8,128)(2,1)} %get-tuple-element.8), kind=kLoop, calls=%fused_computation | loop fusion | bytes 8388608 | tf_op jit(solution)/shard_map/slice | solution.py:700
  118.8 0.0 copy-done
  118.8 0.9 copy.12
Async XLA Ops:
  115.0 3.8 %copy-start = (bf16[768,512]{1,0:T(8,128)(2,1)S(1)}, bf16[768,512]{1,0:T(8,128)(2,1)}, u32[]{:S(2)}) copy-start(bf16[768,512]{1,0:T(8,128)(2,1)} %get-tuple-element.7) | copy-start | bytes 2359300

commit v7 on v6

--- a/solution.py
+++ b/solution.py
@@ -382,9 +382,7 @@
             scale = state[b]["scale"]
             for j in range(3):
                 part = pl.ds(CHUNK * j, CHUNK)
-                p = s_ref[b % 4, part, :] * scale
-                s_ref[b % 4, part, :] = p
-                p_ref[b % 2, part, :] = p.astype(BF16)
+                p_ref[b % 2, part, :] = (s_ref[b % 4, part, :] * scale).astype(BF16)
                 yield
             out_t = nn(vt_ref[feats, pl.ds(CHUNK * c, KEYS)], p_ref[b % 2])
             out_t = out_t.astype(BF16).astype(F32)
@@ -394,11 +392,12 @@
         def gradient(b):
             c, n, feats = parts(b)
             row_dot = state[b]["row_dot"]
+            scale = state[b]["scale"]
             for j in range(3):
                 part = pl.ds(CHUNK * j, CHUNK)
                 rows = pl.ds(starts[c][j], CHUNK)
-                grad_p = nt(v_ref[rows, feats], ubd_ref[b])
-                ds = (s_ref[b % 4, part, :] * (grad_p - row_dot)).astype(BF16)
+                grad_p = nn(v_ref[rows, feats], ubdt_ref[b])
+                ds = (s_ref[b % 4, part, :] * scale * (grad_p - row_dot)).astype(BF16)
                 ds_ref[part, :] = ds
                 gv_ref[rows, feats] += nn(p_ref[b % 2, part, :], ubd_ref[b])
                 gk_ref[rows, feats] += nn(ds, qbd_ref[b])

time: 120 us -> 120 us (level)
  no operation moved by 1% of the time
where the time goes in v7:
time: 120 us
  Pallas kernels  114 us (95%)
  local copies, waits for them, and re-layouts  4.71 us (4%)
    pallas_call x1, Pallas kernels, whole(): pl.pallas_call(kernel, out_shape=(jax.ShapeDtypeStruct((768, D), BF16), j...  114 us
    slice x1, local copies, waits for them, and re-layouts, on_device(): return (grad_tokens, sums[0], sums[1], sums[2], sums[3])  3.82 us

profile of v7, /device:TPU:1, one launch (start us, length us, event | category | flops | bytes accessed | tf_op | source)
XLA Modules:
  0.0 119.6 jit_solution(10200366139536871180)
XLA Ops:
  0.6 114.2 %shard_map.101 = (bf16[768,512]{1,0:T(8,128)(2,1)}, bf16[2048,512]{1,0:T(8,128)(2,1)}) custom-call(bf16[768,512]{1,0:T(8,128)(2,1)} %bitcast.9, bf16[768,512]{1,0:T(8,128)(2,1)} %bitcast.10, bf16[512,512]{1,0:T(8,128)(2,1)} %wq_hbm.1, bf16[512,512]{1,0:T(8,128)(2,1)} %wk_hbm.1, bf16[512,512]{1,0:T(8,128)(2,1)} %wv_hbm.1, bf16[512,512]{1,0:T(8,128)(2,1)} %wo_hbm.1), custom_call_target="tpu_custom_call" | custom-call | tf_op jit(solution)/shard_map/pallas_call | solution.py:678
  114.9 0.0 copy-start
  114.9 3.8 %fusion = (f32[512,512]{1,0:T(8,128)}, f32[512,512]{1,0:T(8,128)}, f32[512,512]{1,0:T(8,128)}, f32[512,512]{1,0:T(8,128)}) fusion(bf16[2048,512]{1,0:T(8,128)(2,1)} %get-tuple-element.8), kind=kLoop, calls=%fused_computation | loop fusion | bytes 8388608 | tf_op jit(solution)/shard_map/slice | solution.py:699
  118.7 0.0 copy-done
  118.7 0.9 copy.12
Async XLA Ops:
  114.9 3.8 %copy-start = (bf16[768,512]{1,0:T(8,128)(2,1)S(1)}, bf16[768,512]{1,0:T(8,128)(2,1)}, u32[]{:S(2)}) copy-start(bf16[768,512]{1,0:T(8,128)(2,1)} %get-tuple-element.7) | copy-start | bytes 2359300
